TPU v7x, 128 devices: a whole 4x4x4 slice. The times are simulated.
128 devices in a mesh: ctx: 8 (over y_lo, x), exp: 16 (over z, y_hi, core).
Axes of the slice: x: 4, y: 4 (y_hi: 2, y_lo: 2; y = y_hi * 2 + y_lo), z: 4, core: 2. Of those that a mesh axis runs over, the one named last changes fastest.
Arguments:
- resid_in: bfloat16 [16384, 2880], P(('exp', 'ctx')), may hold values from -6 to 6
- queries: bfloat16 [16384, 4096], P(('exp', 'ctx')), may hold values from -6 to 6
- keys: bfloat16 [16384, 512], P(('exp', 'ctx')), may hold values from -6 to 6
- values: bfloat16 [16384, 512], P(('exp', 'ctx')), may hold values from -6 to 6
- sinks: float32 [64], replicated, may hold values from 2 to 7
- segments: int32 [16384], P(('exp', 'ctx')), may hold values from 0 to 31, never falling along the last dimension, each value on 1 to 1024 neighbouring positions
- norm_gain: float32 [2880], replicated, may hold values from 0.1 to 1.9
- out_weight: bfloat16 [4096, 2880], P('ctx'), may hold values from -0.75 to 0.75
- gate_weight: bfloat16 [16, 2880, 2880], P('exp', None, 'ctx'), may hold values from -0.109375 to 0.109375
- up_weight: bfloat16 [16, 2880, 2880], P('exp', None, 'ctx'), may hold values from -0.109375 to 0.109375
- down_weight: bfloat16 [16, 2880, 2880], P('exp', 'ctx'), may hold values from -0.109375 to 0.109375
- expert_ids: int32 [16384, 4], P(('exp', 'ctx')), may hold values from 0 to 127, as said below
- route_weights: float32 [16384, 4], P(('exp', 'ctx')), may hold values from 0.1 to 1
Outputs:
- resid_out: bfloat16 [16384, 2880], P(('exp', 'ctx'))
Inputs may be any that keep to these rules, and one draw needn't show every extreme that they name: `expert_ids`: column k of a row names an expert in [k * 32, (k + 1) * 32). Within the rows of one device (aligned blocks of 128 rows) no evaluated expert is named more than 8 times, and one evaluated expert is named exactly 8 times in every block.
All inputs are finite; a program needn't handle non-finite values.
Results may differ from a plain program's by a relative error of at most 0.018.
Values may be sent and summed in bfloat16 or wider, within the bound.
No kernel may reach another device: no remote copies, remote signals or barrier semaphores. Data moves between devices by JAX's collectives and lax.ppermute only.
A program may use at most 128 MiB of HBM per device.

v0:
```python
import functools

import jax
import jax.numpy as jnp
from jax import lax
from jax.experimental import pallas as pl
from jax.experimental.pallas import tpu as pltpu
from jax.sharding import PartitionSpec as P

D = 2880
QUERY_HEADS = 64
KEY_VALUE_HEADS = 8
HEAD_SIZE = 64
ALL_EXPERTS = 128
TOPK = 4
CAP = 8
TOK = 128
FFS = 360
NX = 4
QUARTER = ALL_EXPERTS // TOPK
WINDOW = 4
DOC_ROWS = 16
PACK_ROWS = TOK + DOC_ROWS
PACK_COLS = 1280
HALF = D // 2
MIB = 1024 * 1024

VMEM = pltpu.VMEM
ANY = pl.ANY
SMEM = pltpu.SMEM

RIGHT = [(4 * y + x, 4 * y + (x + 1) % 4) for y in range(2) for x in range(4)]
LEFT = [(4 * y + x, 4 * y + (x + 3) % 4) for y in range(2) for x in range(4)]
FLIP = [(c, c ^ 4) for c in range(8)]

NT = (((1,), (1,)), ((), ()))
TN = (((0,), (0,)), ((), ()))


def go_right(v):
    return lax.ppermute(v, "ctx", RIGHT)


def go_left(v):
    return lax.ppermute(v, "ctx", LEFT)


def go_flip(v):
    return lax.ppermute(v, "ctx", FLIP)


def params(mib):
    return pltpu.CompilerParams(vmem_limit_bytes=mib * MIB)


def spec(space):
    return pl.BlockSpec(memory_space=space)


def add(*pieces):
    total = pieces[0].astype(jnp.float32)
    for piece in pieces[1:]:
        total = total + piece.astype(jnp.float32)
    return total.astype(jnp.bfloat16)


def pack_kernel(q_ref, k_ref, v_ref, seg_ref, out_ref):
    lane = lax.broadcasted_iota(jnp.int32, (TOK, 128), 1)
    docs = jnp.broadcast_to(seg_ref[...].astype(jnp.float32), (DOC_ROWS, 128))
    eighth = jnp.asarray(0.125, jnp.bfloat16)
    for x in range(NX):
        out_ref[x, :TOK, 0:512] = q_ref[:, 512 * x : 512 * x + 512] * eighth
        out_ref[x, :TOK, 512:1024] = q_ref[:, 2048 + 512 * x : 2048 + 512 * x + 512] * eighth
        for ref, start in ((k_ref, 1024), (v_ref, 1152)):
            base = 128 * (x // 2)
            low = ref[:, base : base + 128].astype(jnp.float32)
            high = ref[:, 256 + base : 256 + base + 128].astype(jnp.float32)
            if x % 2 == 0:
                high = pltpu.roll(high, 64, 1)
            else:
                low = pltpu.roll(low, 64, 1)
            out_ref[x, :TOK, start : start + 128] = jnp.where(lane < 64, low, high).astype(
                jnp.bfloat16
            )
        out_ref[x, TOK:, 0:1024] = jnp.zeros((DOC_ROWS, 1024), jnp.bfloat16)
        out_ref[x, TOK:, 1024:1152] = docs.astype(jnp.bfloat16)
        out_ref[x, TOK:, 1152:1280] = jnp.zeros((DOC_ROWS, 128), jnp.bfloat16)


def pack(queries, keys, values, segments):
    return pl.pallas_call(
        pack_kernel,
        out_shape=jax.ShapeDtypeStruct((NX, PACK_ROWS, PACK_COLS), jnp.bfloat16),
        in_specs=[spec(VMEM)] * 4,
        out_specs=spec(VMEM),
        compiler_params=params(10),
        cost_estimate=pl.CostEstimate(flops=0, bytes_accessed=5 << 20, transcendentals=0),
    )(queries, keys, values, segments.reshape(1, TOK))


def attend_kernel(steps, sinks, pack_ref, low_ref, out_ref, key_a, key_b, val_a, val_b, doc_row, bias, hold):
    ctx = lax.axis_index("ctx")
    y, x = ctx // NX, lax.rem(ctx, NX)
    lane = lax.broadcasted_iota(jnp.int32, (TOK, 128), 1)

    def place(ref, b, first, slot):
        rows = pl.ds(pl.multiple_of(slot * TOK, TOK), TOK)
        keys = ref[b, 0:TOK, first : first + 128].astype(jnp.float32)
        vals = ref[b, 0:TOK, first + 128 : first + 256].astype(jnp.float32)
        for g in range(2):
            mine = (lane < 64) if g == 0 else (lane >= 64)
            k_here = jnp.where(mine, keys, 0.0)
            v_here = jnp.where(mine, vals, 1.0)
            k_roll = pltpu.roll(k_here, 64, 1)
            v_roll = pltpu.roll(v_here, 64, 1)
            pair_k = (k_here, k_roll) if g == 0 else (k_roll, k_here)
            pair_v = (v_here, v_roll) if g == 0 else (v_roll, v_here)
            key_a[g, rows] = pair_k[0].astype(jnp.bfloat16)
            key_b[g, rows] = pair_k[1].astype(jnp.bfloat16)
            val_a[g, rows] = pair_v[0].astype(jnp.bfloat16)
            val_b[g, rows] = pair_v[1].astype(jnp.bfloat16)
        doc_row[:, rows] = ref[b, TOK : TOK + 8, first : first + 128].astype(jnp.float32)

    for b in range(NX):
        place(pack_ref, b, 1024, 4 * y + b)

    @pl.when(y == 1)
    def _():
        for b in range(NX):
            place(low_ref, b, 0, b)

    two = 2 * TOK
    upper = lax.broadcasted_iota(jnp.int32, (two, 128), 0) < TOK
    first = lax.broadcasted_iota(jnp.int32, (two, 128), 1) < 64

    def block_rows(index, carry):
        j = lax.rem(x + steps[0] + index * (steps[-1] - steps[0]), NX)
        block = 4 * y + j
        own_docs = doc_row[0:1, pl.ds(pl.multiple_of(block * TOK, TOK), TOK)]
        query_docs = jnp.transpose(jnp.broadcast_to(own_docs, (TOK, TOK)))
        query_place = block * TOK + lax.broadcasted_iota(jnp.int32, (TOK, 128), 0)

        def run(chunks):
            for t in range(2 * chunks):
                cols = slice(128 * t, 128 * t + 128)
                allowed = (query_docs == doc_row[0:1, cols]) & (128 * t + lane <= query_place)
                bias[:, cols] = jnp.where(allowed, 0.0, -jnp.inf)

            def quad(p, carry):
                g = p // 2
                base = pl.multiple_of(p * 256, 256)
                place_out = pl.multiple_of(512 * lax.rem(g + y, 2) + 256 * lax.rem(p, 2), 256)
                q = jnp.concatenate(
                    [
                        pack_ref[j, 0:TOK, pl.ds(base, 128)],
                        pack_ref[j, 0:TOK, pl.ds(pl.multiple_of(base + 128, 128), 128)],
                    ],
                    axis=0,
                )
                head = 8 * x + 32 * g + 4 * lax.rem(p, 2)
                tops, sink_rows = [], []
                for which, key_ref in enumerate((key_a, key_b)):
                    sink = jnp.where(upper, sinks[head + which], sinks[head + 2 + which])
                    top = sink
                    for c in range(chunks):
                        cols = slice(256 * c, 256 * c + 256)
                        s = lax.dot_general(
                            q, key_ref[g, cols], NT, preferred_element_type=jnp.float32
                        )
                        mask = bias[:, cols]
                        s = s + jnp.concatenate([mask, mask], axis=0)
                        hold[which, :, cols] = s
                        top = jnp.maximum(top, jnp.maximum(s[:, 0:128], s[:, 128:256]))
                    tops.append(jnp.max(top, axis=1, keepdims=True))
                    sink_rows.append(sink)
                outs = []
                for which, val_ref in enumerate((val_a, val_b)):
                    total = jnp.zeros((two, 128), jnp.float32)
                    for c in range(chunks):
                        cols = slice(256 * c, 256 * c + 256)
                        prob = jnp.exp(hold[which, :, cols] - tops[which]).astype(jnp.bfloat16)
                        total = total + jnp.dot(
                            prob, val_ref[g, cols], preferred_element_type=jnp.float32
                        )
                    outs.append(total)
                numer = jnp.where(first, outs[0], outs[1])
                divisor = pltpu.roll(jnp.where(first, outs[1], outs[0]), 64, 1)
                gap = jnp.where(first, sink_rows[0] - tops[0], sink_rows[1] - tops[1])
                result = (numer / (divisor + jnp.exp(gap))).astype(jnp.bfloat16)
                rows = pl.ds(pl.multiple_of(index * TOK, TOK), TOK)
                out_ref[rows, pl.ds(place_out, 128)] = result[0:TOK]
                out_ref[rows, pl.ds(pl.multiple_of(place_out + 128, 128), 128)] = result[TOK:]
                return carry

            lax.fori_loop(0, 4, quad, 0)

        for quarter in range(4):

            @pl.when(block // 2 == quarter)
            def _(quarter=quarter):
                run(quarter + 1)

        return carry

    lax.fori_loop(0, len(steps), block_rows, 0)


def attend(steps, sinks, packed, low):
    return pl.pallas_call(
        functools.partial(attend_kernel, steps),
        out_shape=jax.ShapeDtypeStruct((len(steps) * TOK, 1024), jnp.bfloat16),
        in_specs=[spec(SMEM), spec(VMEM), spec(VMEM)],
        out_specs=spec(VMEM),
        scratch_shapes=[
            pltpu.VMEM((2, 1024, 128), jnp.bfloat16),
            pltpu.VMEM((2, 1024, 128), jnp.bfloat16),
            pltpu.VMEM((2, 1024, 128), jnp.bfloat16),
            pltpu.VMEM((2, 1024, 128), jnp.bfloat16),
            pltpu.VMEM((8, 1024), jnp.float32),
            pltpu.VMEM((TOK, 1024), jnp.float32),
            pltpu.VMEM((2, 2 * TOK, 1024), jnp.float32),
        ],
        compiler_params=params(14),
        cost_estimate=pl.CostEstimate(
            flops=2 << 30, bytes_accessed=4 << 20, transcendentals=0
        ),
    )(sinks, packed, low)


def project_kernel(sides, attn, w_own, w_first, w_second, *refs):
    core = lax.rem(lax.axis_index("exp"), 2)
    if sides:
        from_left, from_right, to_right, to_left = refs
    else:
        out_a, out_b = refs
    for part, (w_near, base) in enumerate(((w_first, core * HALF), (w_second, (1 - core) * HALF))):
        for start in range(0, HALF, 288):
            near = slice(start, start + 288)
            rows = pl.ds(pl.multiple_of(base + start, 16), 288)
            total = lax.dot_general(
                w_own[rows], attn[:, 0:512], NT, preferred_element_type=jnp.float32
            ) + lax.dot_general(
                w_near[near], attn[:, 512:1024], NT, preferred_element_type=jnp.float32
            )
            if not sides:
                (out_a, out_b)[part][near] = total.astype(jnp.bfloat16)
                continue
            after, before = total[:, 0:128], total[:, 128:256]
            if part == 0:
                after = after + from_left[near].astype(jnp.float32)
            else:
                before = before + from_right[near].astype(jnp.float32)
            to_right[rows] = after.astype(jnp.bfloat16)
            to_left[rows] = before.astype(jnp.bfloat16)


def project(attn, w_own, w_first, w_second, *extra):
    sides = len(extra) > 0
    rows = D if sides else HALF
    return pl.pallas_call(
        functools.partial(project_kernel, sides),
        out_shape=(jax.ShapeDtypeStruct((rows, TOK), jnp.bfloat16),) * 2,
        in_specs=[spec(VMEM)] * (4 + len(extra)),
        out_specs=(spec(VMEM),) * 2,
        compiler_params=params(10),
        cost_estimate=pl.CostEstimate(flops=3 << 29, bytes_accessed=4 << 20, transcendentals=0),
    )(attn, w_own, w_first, w_second, *extra)


def slot_table(ids):
    local = ids % QUARTER
    chosen = jnp.where(local < WINDOW, ids // QUARTER * WINDOW + local, -1)
    slot = lax.broadcasted_iota(jnp.int32, (TOK, TOK), 0)
    expert = slot // CAP
    hits = [chosen[k : k + 1] == expert for k in range(TOPK)]
    named = functools.reduce(jnp.logical_or, hits)
    before = lax.broadcasted_iota(jnp.int32, (TOK, TOK), 0) < lax.broadcasted_iota(
        jnp.int32, (TOK, TOK), 1
    )
    rank = jnp.dot(
        jnp.where(named, 1.0, 0.0).astype(jnp.bfloat16),
        jnp.where(before, 1.0, 0.0).astype(jnp.bfloat16),
        preferred_element_type=jnp.float32,
    )
    table = named & (rank == (slot % CAP).astype(jnp.float32))
    return table, hits


def norm_kernel(resid, own_a, own_b, left, right, gain, ids, hidden_ref, send_ref, gain_row):
    core = lax.rem(lax.axis_index("exp"), 2)
    gain_row[...] = jnp.ones_like(gain_row)
    gain_row[:, 0:D] = gain[...]
    square = jnp.zeros((8, TOK), jnp.float32)
    for base, own in ((core * HALF, own_a), ((1 - core) * HALF, own_b)):
        for start in range(0, HALF, 160):
            rows = pl.ds(pl.multiple_of(base + start, 16), 160)
            total = own[start : start + 160].astype(jnp.float32)
            total = total + left[rows].astype(jnp.float32) + right[rows].astype(jnp.float32)
            hidden = resid[rows].astype(jnp.float32) + total
            hidden_ref[rows] = hidden
            square = square + jnp.sum((hidden * hidden).reshape(20, 8, TOK), axis=0)
    mean = jnp.sum(square, axis=0, keepdims=True) * (1.0 / D)
    scale = lax.rsqrt(mean + 1e-05)
    table, _ = slot_table(ids[...])
    table = jnp.where(table, 1.0, 0.0).astype(jnp.bfloat16)
    for start in range(0, D, 128):
        size = min(128, D - start)
        rows = slice(start, start + size)
        gains = jnp.transpose(jnp.broadcast_to(gain_row[:, start : start + 128], (128, 128)))
        normed = (hidden_ref[rows] * scale * gains[0:size]).astype(jnp.bfloat16)
        send_ref[:, rows] = lax.dot_general(
            table, normed, NT, preferred_element_type=jnp.float32
        ).astype(jnp.bfloat16)


def norm(resid, own_a, own_b, left, right, gain, ids):
    return pl.pallas_call(
        norm_kernel,
        out_shape=(
            jax.ShapeDtypeStruct((D, TOK), jnp.float32),
            jax.ShapeDtypeStruct((TOK, D), jnp.bfloat16),
        ),
        in_specs=[spec(VMEM)] * 7,
        out_specs=(spec(VMEM), spec(VMEM)),
        scratch_shapes=[pltpu.VMEM((1, D + 64), jnp.float32)],
        compiler_params=params(10),
        cost_estimate=pl.CostEstimate(flops=1 << 27, bytes_accessed=6 << 20, transcendentals=0),
    )(resid, own_a, own_b, left, right, gain, ids)


def combine_kernel(hidden, back, ids, weights, out_ref):
    table, hits = slot_table(ids[...])
    chosen_weight = jnp.zeros((TOK, TOK), jnp.float32)
    for k in range(TOPK):
        chosen_weight = chosen_weight + jnp.where(hits[k], weights[k : k + 1], 0.0)
    share = jnp.where(table, chosen_weight, 0.0)
    high = share.astype(jnp.bfloat16)
    low = (share - high.astype(jnp.float32)).astype(jnp.bfloat16)
    for start in range(0, D, 128):
        cols = slice(start, min(start + 128, D))
        rows = back[:, cols]
        moe = lax.dot_general(rows, high, TN, preferred_element_type=jnp.float32)
        moe = moe + lax.dot_general(rows, low, TN, preferred_element_type=jnp.float32)
        out_ref[cols] = (hidden[cols] + moe).astype(jnp.bfloat16)


def combine(hidden, back, ids, weights):
    return pl.pallas_call(
        combine_kernel,
        out_shape=jax.ShapeDtypeStruct((D, TOK), jnp.bfloat16),
        in_specs=[spec(VMEM)] * 4,
        out_specs=spec(VMEM),
        compiler_params=params(10),
        cost_estimate=pl.CostEstimate(flops=1 << 28, bytes_accessed=3 << 20, transcendentals=0),
    )(hidden, back, ids, weights)


PAIR_DOWN, PAIR_ROWS = 368, 728


def pair_kernel(up, down, out):
    out[0:FFS] = up[...]
    out[FFS:PAIR_DOWN] = jnp.zeros((PAIR_DOWN - FFS, D), jnp.bfloat16)
    out[PAIR_DOWN:PAIR_ROWS] = down[...]


def pair(up, down):
    return pl.pallas_call(
        pair_kernel,
        out_shape=jax.ShapeDtypeStruct((PAIR_ROWS, D), jnp.bfloat16),
        in_specs=[spec(VMEM)] * 2,
        out_specs=spec(VMEM),
        compiler_params=params(10),
        cost_estimate=pl.CostEstimate(flops=0, bytes_accessed=8 << 20, transcendentals=0),
    )(up, down)


def expert_kernel(sizes, near, *refs):
    count = len(sizes)
    core = lax.rem(lax.axis_index("exp"), 2)
    pieces, refs = refs[:count], refs[count:]
    if near:
        gate_0, gate_1, pair_0, pair_1 = refs[:4]
        sums, outs = refs[4 : 4 + count], refs[4 + count : 4 + 2 * count]
        rows_x, gate, up, down, sem = refs[4 + 2 * count :]
        up_rows, down_rows = pl.ds(0, FFS), pl.ds(PAIR_DOWN, FFS)
        fetched = (
            ((gate_0, gate_1), gate),
            ((pair_0.at[up_rows], pair_1.at[up_rows]), up),
            ((pair_0.at[down_rows], pair_1.at[down_rows]), down),
        )
    else:
        (gate, up, down), outs = refs[:3], refs[3 : 3 + count]
        rows_x, sem = refs[3 + count :]
        fetched = ()

    def by_core(index, act):
        for which in range(2 if near else 0):

            @pl.when(core == which)
            def _(which=which):
                sources, held = fetched[index]
                act(pltpu.make_async_copy(sources[which], held, sem.at[count + index]))

    copies = []
    start = 0
    for index, (piece, size) in enumerate(zip(pieces, sizes)):
        copies.append(
            pltpu.make_async_copy(piece, rows_x.at[pl.ds(start, size)], sem.at[index])
        )
        start += size
    for copy in copies:
        copy.start()
    for index in range(len(fetched)):
        by_core(index, lambda copy: copy.start())
    for copy in copies:
        copy.wait()
    x = rows_x[...]
    by_core(0, lambda copy: copy.wait())
    g = lax.dot_general(x, gate[...], NT, preferred_element_type=jnp.float32)
    by_core(1, lambda copy: copy.wait())
    v = lax.dot_general(x, up[...], NT, preferred_element_type=jnp.float32)
    act = ((v + 1.0) * g * jax.nn.sigmoid(1.702 * g)).astype(jnp.bfloat16)
    by_core(2, lambda copy: copy.wait())
    for first in range(0, D, 512):
        cols = slice(first, min(first + 512, D))
        part = jnp.dot(act, down[:, cols], preferred_element_type=jnp.float32)
        start = 0
        for index, (out, size) in enumerate(zip(outs, sizes)):
            here = part[start : start + size]
            if near:
                here = here + sums[index][:, cols].astype(jnp.float32)
            out[:, cols] = here.astype(jnp.bfloat16)
            start += size


def experts(pieces, weights, sums=()):
    sizes = tuple(piece.shape[0] for piece in pieces)
    total = sum(sizes)
    near = len(sums) > 0
    return pl.pallas_call(
        functools.partial(expert_kernel, sizes, near),
        out_shape=tuple(jax.ShapeDtypeStruct((size, D), jnp.bfloat16) for size in sizes),
        in_specs=[spec(ANY)] * len(sizes)
        + [spec(ANY if near else VMEM)] * len(weights)
        + [spec(VMEM)] * len(sums),
        out_specs=tuple(spec(VMEM) for _ in sizes),
        scratch_shapes=[pltpu.VMEM((total, D), jnp.bfloat16)]
        + [pltpu.VMEM((FFS, D), jnp.bfloat16)] * (3 if near else 0)
        + [pltpu.SemaphoreType.DMA((len(sizes) + 3,))],
        compiler_params=params(16 if near else 10),
        cost_estimate=pl.CostEstimate(
            flops=6 * total * D * FFS, bytes_accessed=4 << 20, transcendentals=0
        ),
    )(*pieces, *weights, *sums)


def over_all(move):
    pairs = []
    for c in range(8):
        for e in range(16):
            y, x, z, hi, core = move(c // 4, c % 4, e // 4, e // 2 % 2, e % 2)
            pairs.append((c * 16 + e, (y * 4 + x) * 16 + z * 4 + hi * 2 + core))
    return pairs


def partner(y, x, z, hi, core):
    return (1 - y, x, z, hi, core) if core == 0 else (y, x ^ 1, z, hi, core)


def onward(y, x, z, hi, core):
    if core == 0:
        return y, (x + 1) % 4, z, hi, core
    across = x < 2 if y == 0 else x >= 2
    return (y, 3 - x, z, hi, core) if across else (1 - y, x, z, hi, core)


def across_y(y, x, z, hi, core):
    place = (2 * hi + y + (1 if y == 1 else 3)) % 4
    return place % 2, x, z, place // 2, core


def permute(v, pairs):
    return lax.ppermute(v, ("ctx", "exp"), pairs)


NEXT = over_all(onward)
BACK = [(b, a) for a, b in NEXT]
PARTNER = over_all(partner)
PARTNER_0 = [(a, b if a % 2 == 0 else a) for a, b in PARTNER]
PARTNER_1 = [(a, b if a % 2 == 1 else a) for a, b in PARTNER]
ACROSS = over_all(across_y)
SWAP = over_all(lambda y, x, z, hi, core: (y, x, z, hi, 1 - core))


def exchange_experts(arrived, own, near):
    half = TOK // 2
    own_a, own_b = arrived[:half], arrived[half:]
    prev_a, next_b = permute(own_a, NEXT), permute(own_b, BACK)
    prev_b, next_a = permute(own_b, NEXT), permute(own_a, BACK)
    opp_a, opp_b = permute(prev_a, NEXT), permute(next_b, BACK)
    early = (own_a, own_b, prev_a, next_b)
    early_sums = experts(early, own)
    late = (opp_a, opp_b, prev_b, next_a)
    late, early_sums = lax.optimization_barrier((late, early_sums))
    late_sums = experts(late, own)
    near, late_sums = lax.optimization_barrier((near, late_sums))
    far_a, far_b, op_b, on_a = experts(late, near, late_sums)
    far_a, far_b, op_b, on_a, early, early_sums = lax.optimization_barrier(
        (far_a, far_b, op_b, on_a, early, early_sums)
    )
    far_a, far_b = permute(far_a, NEXT), permute(far_b, BACK)
    oo_a, oo_b, op_a, on_b = experts(early, near, early_sums)
    far_a, far_b, oo_a, oo_b, op_a, on_b = lax.optimization_barrier(
        (far_a, far_b, oo_a, oo_b, op_a, on_b)
    )
    from_prev = permute(jnp.stack([add(on_a, far_a), on_b]), NEXT)
    from_next = permute(jnp.stack([op_a, add(op_b, far_b)]), BACK)
    out_a, out_b = add(oo_a, from_prev[0], from_next[0]), add(oo_b, from_prev[1], from_next[1])
    return jnp.concatenate([out_a, out_b], axis=0)


def on_device(
    resid_in,
    queries,
    keys,
    values,
    sinks,
    segments,
    norm_gain,
    out_weight,
    gate_weight,
    up_weight,
    down_weight,
    expert_ids,
    route_weights,
):
    core = lax.axis_index("exp") % 2
    gate, up, down = gate_weight[0].T, up_weight[0].T, down_weight[0]
    w_own = out_weight.T

    mine = lax.dynamic_slice_in_dim(w_own, core * HALF, HALF, 0)
    mine, gate_out = lax.optimization_barrier((mine, gate))
    w_first = permute(mine, ACROSS)
    gate_0 = permute(gate_out, PARTNER_0)

    packed = pack(queries, keys, values, segments)
    packed = lax.all_to_all(
        packed,
        "ctx",
        split_axis=0,
        concat_axis=0,
        tiled=True,
        axis_index_groups=[[0, 1, 2, 3], [4, 5, 6, 7]],
    )
    packed, gate_0, gate_out = lax.optimization_barrier((packed, gate_0, gate))
    low = lax.ppermute(packed[:, :, 1024:], "ctx", [(x, x + 4) for x in range(4)])
    gate_1 = permute(gate_out, PARTNER_1)
    both = pair(up, down)
    low, w_first, both = lax.optimization_barrier((low, w_first, both))
    w_second = permute(w_first, SWAP)
    pair_0 = permute(both, PARTNER_0)

    weights = (w_own, w_first, w_second)
    opp_a, opp_b = project(attend((2,), sinks, packed, low), *weights)
    opp_a, opp_b, packed, low = lax.optimization_barrier((opp_a, opp_b, packed, low))
    from_left, from_right = go_right(opp_a), go_left(opp_b)
    attn = attend((1, 3), sinks, packed, low)
    attn, gate_1 = lax.optimization_barrier((attn, gate_1))
    to_right, to_left = project(attn, *weights, from_left, from_right)
    to_right, to_left, packed, low = lax.optimization_barrier((to_right, to_left, packed, low))
    left, right = go_right(to_right), go_left(to_left)
    own_a, own_b = project(attend((0,), sinks, packed, low), *weights)
    left, right, own_a, own_b, both = lax.optimization_barrier((left, right, own_a, own_b, both))
    pair_1 = permute(both, PARTNER_1)

    ids = expert_ids.T
    hidden, send = norm(
        resid_in.T, own_a, own_b, left, right, norm_gain.reshape(1, D), ids
    )
    arrived = lax.all_to_all(send, "exp", split_axis=0, concat_axis=0, tiled=True)
    arrived, pair_0 = lax.optimization_barrier((arrived, pair_0))
    summed = exchange_experts(arrived, (gate, up, down), (gate_0, gate_1, pair_0, pair_1))
    back = lax.all_to_all(summed, "exp", split_axis=0, concat_axis=0, tiled=True)
    return combine(hidden, back, ids, route_weights.T).T


def solution(mesh):
    placed = (
        P(("exp", "ctx"), None),
        P(("exp", "ctx"), None),
        P(("exp", "ctx"), None),
        P(("exp", "ctx"), None),
        P(),
        P(("exp", "ctx")),
        P(),
        P("ctx", None),
        P("exp", None, "ctx"),
        P("exp", None, "ctx"),
        P("exp", "ctx", None),
        P(("exp", "ctx"), None),
        P(("exp", "ctx"), None),
    )
    return jax.shard_map(
        on_device, mesh=mesh, in_specs=placed, out_specs=P(("exp", "ctx"), None), check_vma=False
    )
```

profile of v0, /device:TPU:1, one launch (start us, length us, event | category | flops | bytes accessed | tf_op | source)
XLA Modules:
  0.0 202.2 jit_solution(16560254705814837023)
XLA Ops:
  0.0 1.6 dynamic-slice_bitcast_fusion
  1.7 0.4 copy-done.3
  2.0 0.8 collective-permute-start
  2.8 3.6 %collective-permute-start.2 = (bf16[1440,512]{1,0:T(8,128)(2,1)S(1)}, bf16[1440,512]{1,0:T(8,128)(2,1)S(1)}, u32[]{:S(2)}, u32[]{:S(2)}) collective-permute-start(bf16[1440,512]{1,0:T(8,128)(2,1)S(1)} %dynamic-slice_bitcast_fusion), channel_id=1, source_target_pairs={{0,66},{1,67},{2,64},{3,65},{4,70},{5,71},{6,68},{7,69},{8,74},{9,... | collective-permute-start | bytes 4423688 | tf_op jit(solution)/shard_map/ppermute | solution.py:484
  6.5 1.2 copy-done.4
  7.7 0.2 shard_map.127
  7.9 0.0 copy-start.1
  8.0 20.5 %all_to_all.28.pack_ref = bf16[4,144,1280]{2,1,0:T(8,128)(2,1)S(1)} all-to-all(bf16[4,144,1280]{2,1,0:T(8,128)(2,1)S(1)} %shard_map.127), channel_id=1, replica_groups={{0,16,32,48},{64,80,96,112},{1,17,33,49},{65,81,97,113},{2,18,34,50},{6..., dimensions={0} | all-to-all | bytes 2949120 | tf_op jit(solution)/shard_map/all_to_all | solution.py:548
  28.5 1.3 collective-permute-start.1
  29.8 2.3 %collective-permute-start.4 = (bf16[360,2880]{1,0:T(8,128)(2,1)S(1)}, bf16[360,2880]{1,0:T(8,128)(2,1)S(1)}, u32[]{:S(2)}, u32[]{:S(2)}) collective-permute-start(bf16[360,2880]{1,0:T(8,128)(2,1)S(1)} %bitcast.56), channel_id=1, source_target_pairs={{0,0},{1,17},{2,2},{3,19},{4,4},{5,21},{6,6},{7,23},{8,8},{9,25},{... | collective-permute-start | bytes 6220808 | tf_op jit(solution)/shard_map/ppermute | solution.py:484
  32.2 0.0 copy-start.11
  32.2 0.3 shard_map.128
  32.5 0.0 copy-start
  32.5 3.0 %collective-permute-done.2.w_first = bf16[1440,512]{1,0:T(8,128)(2,1)S(1)} collective-permute-done((bf16[1440,512]{1,0:T(8,128)(2,1)S(1)}, bf16[1440,512]{1,0:T(8,128)(2,1)S(1)}, u32[]{:S(2)}, u32[]{:S(2)}) %collective-permute-start.2) | collective-permute-done | bytes 1474592 | tf_op jit(solution)/shard_map/ppermute | solution.py:484
  35.5 4.2 %collective-permute-start.3 = (bf16[1440,512]{1,0:T(8,128)(2,1)S(1)}, bf16[1440,512]{1,0:T(8,128)(2,1)S(1)}, u32[]{:S(2)}, u32[]{:S(2)}) collective-permute-start(bf16[1440,512]{1,0:T(8,128)(2,1)S(1)} %collective-permute-done.2.w_first), channel_id=1, source_target_pairs={{0,1},{1,0},{2,3},{3,2},{4,5},{5,4},{6,7},{7,6},{8,9},{9,8},{10,11... | collective-permute-start | bytes 4423688 | tf_op jit(solution)/shard_map/ppermute | solution.py:484
  39.7 0.9 collective-permute-start.9
  40.7 3.5 %shard_map.129.attn = bf16[128,1024]{1,0:T(8,128)(2,1)S(1)} custom-call(f32[64]{0:T(128)S(1)} %copy-done.11, bf16[4,144,1280]{2,1,0:T(8,128)(2,1)S(1)} %all_to_all.28.pack_ref, bf16[4,144,256]{2,1,0:T(8,128)(2,1)S(1)} %collective-permute-done.1.low_ref), custom_call_target="tpu_custom_call" | custom-call | flops 2147483648 | bytes 4194304 | tf_op jit(solution)/shard_map/pallas_call | solution.py:209
  44.2 1.7 shard_map.130
  45.9 1.8 collective-permute-start.5
  47.7 1.7 collective-permute-start.6
  49.4 6.0 %shard_map.131.attn = bf16[256,1024]{1,0:T(8,128)(2,1)S(1)} custom-call(f32[64]{0:T(128)S(1)} %copy-done.11, bf16[4,144,1280]{2,1,0:T(8,128)(2,1)S(1)} %all_to_all.28.pack_ref, bf16[4,144,256]{2,1,0:T(8,128)(2,1)S(1)} %collective-permute-done.1.low_ref), custom_call_target="tpu_custom_call" | custom-call | flops 2147483648 | bytes 4194304 | tf_op jit(solution)/shard_map/pallas_call | solution.py:209
  55.4 4.1 %collective-permute-done.4.refs_5_ = bf16[360,2880]{1,0:T(8,128)(2,1)S(1)} collective-permute-done((bf16[360,2880]{1,0:T(8,128)(2,1)S(1)}, bf16[360,2880]{1,0:T(8,128)(2,1)S(1)}, u32[]{:S(2)}, u32[]{:S(2)}) %collective-permute-start.4) | collective-permute-done | bytes 2073632 | tf_op jit(solution)/shard_map/ppermute | solution.py:484
  59.5 3.8 %collective-permute-done.5.refs_0_ = bf16[1440,128]{1,0:T(8,128)(2,1)S(1)} collective-permute-done((bf16[1440,128]{1,0:T(8,128)(2,1)S(1)}, bf16[1440,128]{1,0:T(8,128)(2,1)S(1)}, u32[]{:S(2)}, u32[]{:S(2)}) %collective-permute-start.5) | collective-permute-done | bytes 368672 | tf_op jit(solution)/shard_map/ppermute | solution.py:41
  63.3 1.8 collective-permute-done.6.refs_1_
  65.0 1.8 shard_map.132
  66.9 0.5 collective-permute-start.7
  67.4 2.2 %collective-permute-start.8 = (bf16[2880,128]{1,0:T(8,128)(2,1)S(1)}, bf16[2880,128]{1,0:T(8,128)(2,1)S(1)}, u32[]{:S(2)}, u32[]{:S(2)}) collective-permute-start(bf16[2880,128]{1,0:T(8,128)(2,1)S(1)} %get-tuple-element.104), channel_id=1, source_target_pairs={{0,48},{16,0},{32,16},{48,32},{64,112},{80,64},{96,80},{112,96},{1... | collective-permute-start | bytes 2211848 | tf_op jit(solution)/shard_map/ppermute | solution.py:45
  69.6 3.0 %shard_map.133.attn = bf16[128,1024]{1,0:T(8,128)(2,1)S(1)} custom-call(f32[64]{0:T(128)S(1)} %copy-done.11, bf16[4,144,1280]{2,1,0:T(8,128)(2,1)S(1)} %all_to_all.28.pack_ref, bf16[4,144,256]{2,1,0:T(8,128)(2,1)S(1)} %collective-permute-done.1.low_ref), custom_call_target="tpu_custom_call" | custom-call | flops 2147483648 | bytes 4194304 | tf_op jit(solution)/shard_map/pallas_call | solution.py:209
  72.7 1.7 shard_map.134
  74.4 10.5 %collective-permute-done.7.left = bf16[2880,128]{1,0:T(8,128)(2,1)S(1)} collective-permute-done((bf16[2880,128]{1,0:T(8,128)(2,1)S(1)}, bf16[2880,128]{1,0:T(8,128)(2,1)S(1)}, u32[]{:S(2)}, u32[]{:S(2)}) %collective-permute-start.7) | collective-permute-done | bytes 737312 | tf_op jit(solution)/shard_map/ppermute | solution.py:41
  84.9 2.4 %collective-permute-start.16 = (bf16[728,2880]{1,0:T(8,128)(2,1)S(1)}, bf16[728,2880]{1,0:T(8,128)(2,1)S(1)}, u32[]{:S(2)}, u32[]{:S(2)}) collective-permute-start(bf16[728,2880]{1,0:T(8,128)(2,1)S(1)} %shard_map.128), channel_id=1, source_target_pairs={{0,0},{1,17},{2,2},{3,19},{4,4},{5,21},{6,6},{7,23},{8,8},{9,25},{... | collective-permute-start | bytes 12579848 | tf_op jit(solution)/shard_map/ppermute | solution.py:484
  87.4 1.1 shard_map.135
  88.5 20.2 %all_to_all.29 = bf16[16,8,2880]{2,1,0:T(8,128)(2,1)S(1)} all-to-all(bf16[16,8,2880]{2,1,0:T(8,128)(2,1)S(1)} %bitcast.60), channel_id=1, replica_groups=mesh['ctx'=8,'exp'=16] {'exp'}, dimensions={0} | all-to-all | bytes 1474560 | tf_op jit(solution)/shard_map/all_to_all | solution.py:581
  108.7 0.1 fusion.4
  108.8 0.1 collective-permute-start.12
  108.9 2.7 %collective-permute-start.10 = (bf16[64,2880]{1,0:T(8,128)(2,1)S(1)}, bf16[64,2880]{1,0:T(8,128)(2,1)S(1)}, u32[]{:S(2)}, u32[]{:S(2)}) collective-permute-start(bf16[64,2880]{1,0:T(8,128)(2,1)S(1)} %get-tuple-element.151.refs_0_), channel_id=1, source_target_pairs={{0,16},{1,49},{2,18},{3,51},{4,20},{5,53},{6,22},{7,55},{8,24},{9,... | collective-permute-start | bytes 1105928 | tf_op jit(solution)/shard_map/ppermute | solution.py:484
  111.6 1.4 collective-permute-start.14
  113.0 0.1 collective-permute-start.15
  113.1 3.4 %collective-permute-done.12.refs_3_ = bf16[64,2880]{1,0:T(8,128)(2,1)S(1)} collective-permute-done((bf16[64,2880]{1,0:T(8,128)(2,1)S(1)}, bf16[64,2880]{1,0:T(8,128)(2,1)S(1)}, u32[]{:S(2)}, u32[]{:S(2)}) %collective-permute-start.12) | collective-permute-done | bytes 368672 | tf_op jit(solution)/shard_map/ppermute | solution.py:484
  116.5 1.3 collective-permute-start.13
  117.9 1.1 collective-permute-done.10.refs_2_
  118.9 3.4 %collective-permute-start.11 = (bf16[64,2880]{1,0:T(8,128)(2,1)S(1)}, bf16[64,2880]{1,0:T(8,128)(2,1)S(1)}, u32[]{:S(2)}, u32[]{:S(2)}) collective-permute-start(bf16[64,2880]{1,0:T(8,128)(2,1)S(1)} %collective-permute-done.10.refs_2_), channel_id=1, source_target_pairs={{0,16},{1,49},{2,18},{3,51},{4,20},{5,53},{6,22},{7,55},{8,24},{9,... | collective-permute-start | bytes 1105928 | tf_op jit(solution)/shard_map/ppermute | solution.py:484
  122.3 3.4 %shard_map.136 = (bf16[64,2880]{1,0:T(8,128)(2,1)S(1)}, bf16[64,2880]{1,0:T(8,128)(2,1)S(1)}, bf16[64,2880]{1,0:T(8,128)(2,1)S(1)}, bf16[64,2880]{1,0:T(8,128)(2,1)S(1)}) custom-call(bf16[64,2880]{1,0:T(8,128)(2,1)S(1)} %get-tuple-element.151.refs_0_, bf16[64,2880]{1,0:T(8,128)(2,1)S(1)} %get-tuple-element.152.refs_1_, ...), custom_call_target="tpu_custom_call" | custom-call | flops 1592524800 | bytes 4194304 | tf_op jit(solution)/shard_map/pallas_call | solution.py:441
  125.7 1.3 collective-permute-done.14.refs_2_
  127.0 5.9 %collective-permute-done.13.refs_1_ = bf16[64,2880]{1,0:T(8,128)(2,1)S(1)} collective-permute-done((bf16[64,2880]{1,0:T(8,128)(2,1)S(1)}, bf16[64,2880]{1,0:T(8,128)(2,1)S(1)}, u32[]{:S(2)}, u32[]{:S(2)}) %collective-permute-start.13) | collective-permute-done | bytes 368672 | tf_op jit(solution)/shard_map/ppermute | solution.py:484
  132.9 2.1 %collective-permute-done.11.refs_0_ = bf16[64,2880]{1,0:T(8,128)(2,1)S(1)} collective-permute-done((bf16[64,2880]{1,0:T(8,128)(2,1)S(1)}, bf16[64,2880]{1,0:T(8,128)(2,1)S(1)}, u32[]{:S(2)}, u32[]{:S(2)}) %collective-permute-start.11) | collective-permute-done | bytes 368672 | tf_op jit(solution)/shard_map/ppermute | solution.py:484
  135.1 3.4 %shard_map.137 = (bf16[64,2880]{1,0:T(8,128)(2,1)S(1)}, bf16[64,2880]{1,0:T(8,128)(2,1)S(1)}, bf16[64,2880]{1,0:T(8,128)(2,1)S(1)}, bf16[64,2880]{1,0:T(8,128)(2,1)S(1)}) custom-call(bf16[64,2880]{1,0:T(8,128)(2,1)S(1)} %collective-permute-done.11.refs_0_, bf16[64,2880]{1,0:T(8,128)(2,1)S(1)} %collective-permute-done.13.refs_1_, ...), custom_call_target="tpu_custom_call" | custom-call | flops 1592524800 | bytes 4194304 | tf_op jit(solution)/shard_map/pallas_call | solution.py:441
  138.5 8.7 %collective-permute-done.16.refs_7_ = bf16[728,2880]{1,0:T(8,128)(2,1)S(1)} collective-permute-done((bf16[728,2880]{1,0:T(8,128)(2,1)S(1)}, bf16[728,2880]{1,0:T(8,128)(2,1)S(1)}, u32[]{:S(2)}, u32[]{:S(2)}) %collective-permute-start.16) | collective-permute-done | bytes 4193312 | tf_op jit(solution)/shard_map/ppermute | solution.py:484
  147.2 4.3 %shard_map.138 = (bf16[64,2880]{1,0:T(8,128)(2,1)S(1)}, bf16[64,2880]{1,0:T(8,128)(2,1)S(1)}, bf16[64,2880]{1,0:T(8,128)(2,1)S(1)}, bf16[64,2880]{1,0:T(8,128)(2,1)S(1)}) custom-call(bf16[64,2880]{1,0:T(8,128)(2,1)S(1)} %collective-permute-done.11.refs_0_, bf16[64,2880]{1,0:T(8,128)(2,1)S(1)} %collective-permute-done.13.refs_1_, ...), custom_call_target="tpu_custom_call" | custom-call | flops 1592524800 | bytes 4194304 | tf_op jit(solution)/shard_map/pallas_call | solution.py:441
  151.5 3.0 %collective-permute-start.17 = (bf16[64,2880]{1,0:T(8,128)(2,1)S(1)}, bf16[64,2880]{1,0:T(8,128)(2,1)S(1)}, u32[]{:S(2)}, u32[]{:S(2)}) collective-permute-start(bf16[64,2880]{1,0:T(8,128)(2,1)S(1)} %get-tuple-element.149), channel_id=1, source_target_pairs={{0,16},{1,49},{2,18},{3,51},{4,20},{5,53},{6,22},{7,55},{8,24},{9,... | collective-permute-start | bytes 1105928 | tf_op jit(solution)/shard_map/ppermute | solution.py:484
  154.6 4.3 %shard_map.139 = (bf16[64,2880]{1,0:T(8,128)(2,1)S(1)}, bf16[64,2880]{1,0:T(8,128)(2,1)S(1)}, bf16[64,2880]{1,0:T(8,128)(2,1)S(1)}, bf16[64,2880]{1,0:T(8,128)(2,1)S(1)}) custom-call(bf16[64,2880]{1,0:T(8,128)(2,1)S(1)} %get-tuple-element.151.refs_0_, bf16[64,2880]{1,0:T(8,128)(2,1)S(1)} %get-tuple-element.152.refs_1_, ...), custom_call_target="tpu_custom_call" | custom-call | flops 1592524800 | bytes 4194304 | tf_op jit(solution)/shard_map/pallas_call | solution.py:441
  158.9 0.2 collective-permute-done.17
  159.1 3.1 %collective-permute-done.18 = bf16[64,2880]{1,0:T(8,128)(2,1)S(1)} collective-permute-done((bf16[64,2880]{1,0:T(8,128)(2,1)S(1)}, bf16[64,2880]{1,0:T(8,128)(2,1)S(1)}, u32[]{:S(2)}, u32[]{:S(2)}) %collective-permute-start.18) | collective-permute-done | bytes 368672 | tf_op jit(solution)/shard_map/ppermute | solution.py:484
  162.2 0.1 fusion.3
  162.3 0.1 pad_maximum_fusion.1
  162.4 0.1 collective-permute-start.20
  162.5 0.1 fusion.2
  162.6 0.1 pad_maximum_fusion
  162.7 2.7 %collective-permute-start.19 = (bf16[2,64,2880]{2,1,0:T(8,128)(2,1)S(1)}, bf16[2,64,2880]{2,1,0:T(8,128)(2,1)S(1)}, u32[]{:S(2)}, u32[]{:S(2)}) collective-permute-start(bf16[2,64,2880]{2,1,0:T(8,128)(2,1)S(1)} %pad_maximum_fusion), channel_id=1, source_target_pairs={{0,16},{1,49},{2,18},{3,51},{4,20},{5,53},{6,22},{7,55},{8,24},{9,... | collective-permute-start | bytes 2211848 | tf_op jit(solution)/shard_map/ppermute | solution.py:484
  165.4 13.3 %collective-permute-done.20 = bf16[2,64,2880]{2,1,0:T(8,128)(2,1)S(1)} collective-permute-done((bf16[2,64,2880]{2,1,0:T(8,128)(2,1)S(1)}, bf16[2,64,2880]{2,1,0:T(8,128)(2,1)S(1)}, u32[]{:S(2)}, u32[]{:S(2)}) %collective-permute-start.20) | collective-permute-done | bytes 737312 | tf_op jit(solution)/shard_map/ppermute | solution.py:484
  178.7 0.3 fusion.1
  179.0 0.1 maximum_bitcast_fusion
  179.1 21.5 %all_to_all.30 = bf16[16,8,2880]{2,1,0:T(8,128)(2,1)S(1)} all-to-all(bf16[16,8,2880]{2,1,0:T(8,128)(2,1)S(1)} %maximum_bitcast_fusion), channel_id=1, replica_groups=mesh['ctx'=8,'exp'=16] {'exp'}, dimensions={0} | all-to-all | bytes 1474560 | tf_op jit(solution)/shard_map/all_to_all | solution.py:584
  200.6 1.6 shard_map.140
  (31 shorter events, 0.1 us)
Async XLA Ops:
  0.0 2.0 %copy-start.3 = (bf16[1,2880,360]{1,2,0:T(8,128)(2,1)S(1)}, bf16[1,2880,360]{1,2,0:T(8,128)(2,1)}, u32[]{:S(2)}) copy-start(bf16[1,2880,360]{1,2,0:T(8,128)(2,1)} %param.21) | copy-start | bytes 6220804
  0.0 6.5 %copy-start.10 = (s32[128]{0:T(128)S(1)}, s32[128]{0:T(128)}, u32[]{:S(2)}) copy-start(s32[128]{0:T(128)} %param.18) | copy-start | bytes 1540
  0.0 6.5 %copy-start.7 = (bf16[128,512]{1,0:T(8,128)(2,1)S(1)}, bf16[128,512]{1,0:T(8,128)(2,1)}, u32[]{:S(2)}) copy-start(bf16[128,512]{1,0:T(8,128)(2,1)} %v_ref.1) | copy-start | bytes 393220
  0.0 6.5 %copy-start.6 = (bf16[128,512]{1,0:T(8,128)(2,1)S(1)}, bf16[128,512]{1,0:T(8,128)(2,1)}, u32[]{:S(2)}) copy-start(bf16[128,512]{1,0:T(8,128)(2,1)} %k_ref.1) | copy-start | bytes 393220
  2.0 26.5 %collective-permute-start = (bf16[360,2880]{1,0:T(8,128)(2,1)S(1)}, bf16[360,2880]{1,0:T(8,128)(2,1)S(1)}, u32[]{:S(2)}, u32[]{:S(2)}) collective-permute-start(bf16[360,2880]{1,0:T(8,128)(2,1)S(1)} %bitcast.55), channel_id=1, source_target_pairs={{0,64},{1,1},{2,66},{3,3},{4,68},{5,5},{6,70},{7,7},{8,72},{9,9},{... | collective-permute-start | bytes 6220808 | tf_op jit(solution)/shard_map/ppermute | solution.py:484
  2.8 32.7 %collective-permute-start.2 = (bf16[1440,512]{1,0:T(8,128)(2,1)S(1)}, bf16[1440,512]{1,0:T(8,128)(2,1)S(1)}, u32[]{:S(2)}, u32[]{:S(2)}) collective-permute-start(bf16[1440,512]{1,0:T(8,128)(2,1)S(1)} %dynamic-slice_bitcast_fusion), channel_id=1, source_target_pairs={{0,66},{1,67},{2,64},{3,65},{4,70},{5,71},{6,68},{7,69},{8,74},{9,... | collective-permute-start | bytes 4423688 | tf_op jit(solution)/shard_map/ppermute | solution.py:484
  6.5 1.2 copy-start.4
  7.7 24.5 %copy-start.2 = (bf16[1,360,2880]{2,1,0:T(8,128)(2,1)S(1)}, bf16[1,360,2880]{2,1,0:T(8,128)(2,1)}, u32[]{:S(2)}) copy-start(bf16[1,360,2880]{2,1,0:T(8,128)(2,1)} %param.23) | copy-start | bytes 6220804
  7.9 24.2 %copy-start.1 = (bf16[1,2880,360]{1,2,0:T(8,128)(2,1)S(1)}, bf16[1,2880,360]{1,2,0:T(8,128)(2,1)}, u32[]{:S(2)}) copy-start(bf16[1,2880,360]{1,2,0:T(8,128)(2,1)} %param.22) | copy-start | bytes 6220804
  28.5 7.0 %collective-permute-start.1 = (bf16[4,144,256]{2,1,0:T(8,128)(2,1)S(1)}, bf16[4,144,256]{2,1,0:T(8,128)(2,1)S(1)}, u32[]{:S(2)}, u32[]{:S(2)}) collective-permute-start(bf16[4,144,256]{2,1,0:T(8,128)(2,1)S(1)} %slice.21), channel_id=1, source_target_pairs={{0,64},{16,80},{32,96},{48,112},{1,65},{17,81},{33,97},{49,113},{2... | collective-permute-start | bytes 884744 | tf_op jit(solution)/shard_map/ppermute | solution.py:557
  29.8 29.7 %collective-permute-start.4 = (bf16[360,2880]{1,0:T(8,128)(2,1)S(1)}, bf16[360,2880]{1,0:T(8,128)(2,1)S(1)}, u32[]{:S(2)}, u32[]{:S(2)}) collective-permute-start(bf16[360,2880]{1,0:T(8,128)(2,1)S(1)} %bitcast.56), channel_id=1, source_target_pairs={{0,0},{1,17},{2,2},{3,19},{4,4},{5,21},{6,6},{7,23},{8,8},{9,25},{... | collective-permute-start | bytes 6220808 | tf_op jit(solution)/shard_map/ppermute | solution.py:484
  32.2 8.5 %copy-start.11 = (f32[64]{0:T(128)S(1)}, f32[64]{0:T(128)}, u32[]{:S(2)}) copy-start(f32[64]{0:T(128)} %sinks.5) | copy-start | bytes 772
  32.5 11.7 %copy-start = (bf16[512,2880]{0,1:T(8,128)(2,1)S(1)}, bf16[512,2880]{0,1:T(8,128)(2,1)}, u32[]{:S(2)}) copy-start(bf16[512,2880]{0,1:T(8,128)(2,1)} %param.20) | copy-start | bytes 8847364
  35.5 8.6 %collective-permute-start.3 = (bf16[1440,512]{1,0:T(8,128)(2,1)S(1)}, bf16[1440,512]{1,0:T(8,128)(2,1)S(1)}, u32[]{:S(2)}, u32[]{:S(2)}) collective-permute-start(bf16[1440,512]{1,0:T(8,128)(2,1)S(1)} %collective-permute-done.2.w_first), channel_id=1, source_target_pairs={{0,1},{1,0},{2,3},{3,2},{4,5},{5,4},{6,7},{7,6},{8,9},{9,8},{10,11... | collective-permute-start | bytes 4423688 | tf_op jit(solution)/shard_map/ppermute | solution.py:484
  39.7 69.0 %collective-permute-start.9 = (bf16[728,2880]{1,0:T(8,128)(2,1)S(1)}, bf16[728,2880]{1,0:T(8,128)(2,1)S(1)}, u32[]{:S(2)}, u32[]{:S(2)}) collective-permute-start(bf16[728,2880]{1,0:T(8,128)(2,1)S(1)} %shard_map.128), channel_id=1, source_target_pairs={{0,64},{1,1},{2,66},{3,3},{4,68},{5,5},{6,70},{7,7},{8,72},{9,9},{... | collective-permute-start | bytes 12579848 | tf_op jit(solution)/shard_map/ppermute | solution.py:484
  45.9 17.4 %collective-permute-start.5 = (bf16[1440,128]{1,0:T(8,128)(2,1)S(1)}, bf16[1440,128]{1,0:T(8,128)(2,1)S(1)}, u32[]{:S(2)}, u32[]{:S(2)}) collective-permute-start(bf16[1440,128]{1,0:T(8,128)(2,1)S(1)} %get-tuple-element.99), channel_id=1, source_target_pairs={{0,16},{16,32},{32,48},{48,0},{64,80},{80,96},{96,112},{112,64},{1... | collective-permute-start | bytes 1105928 | tf_op jit(solution)/shard_map/ppermute | solution.py:41
  47.7 17.3 %collective-permute-start.6 = (bf16[1440,128]{1,0:T(8,128)(2,1)S(1)}, bf16[1440,128]{1,0:T(8,128)(2,1)S(1)}, u32[]{:S(2)}, u32[]{:S(2)}) collective-permute-start(bf16[1440,128]{1,0:T(8,128)(2,1)S(1)} %get-tuple-element.100), channel_id=1, source_target_pairs={{0,48},{16,0},{32,16},{48,32},{64,112},{80,64},{96,80},{112,96},{1... | collective-permute-start | bytes 1105928 | tf_op jit(solution)/shard_map/ppermute | solution.py:45
  66.9 18.0 %collective-permute-start.7 = (bf16[2880,128]{1,0:T(8,128)(2,1)S(1)}, bf16[2880,128]{1,0:T(8,128)(2,1)S(1)}, u32[]{:S(2)}, u32[]{:S(2)}) collective-permute-start(bf16[2880,128]{1,0:T(8,128)(2,1)S(1)} %get-tuple-element.103), channel_id=1, source_target_pairs={{0,16},{16,32},{32,48},{48,0},{64,80},{80,96},{96,112},{112,64},{1... | collective-permute-start | bytes 2211848 | tf_op jit(solution)/shard_map/ppermute | solution.py:41
  67.4 17.5 %collective-permute-start.8 = (bf16[2880,128]{1,0:T(8,128)(2,1)S(1)}, bf16[2880,128]{1,0:T(8,128)(2,1)S(1)}, u32[]{:S(2)}, u32[]{:S(2)}) collective-permute-start(bf16[2880,128]{1,0:T(8,128)(2,1)S(1)} %get-tuple-element.104), channel_id=1, source_target_pairs={{0,48},{16,0},{32,16},{48,32},{64,112},{80,64},{96,80},{112,96},{1... | collective-permute-start | bytes 2211848 | tf_op jit(solution)/shard_map/ppermute | solution.py:45
  72.7 14.7 %copy-start.12 = (f32[2880]{0:T(1024)S(1)}, f32[2880]{0:T(1024)}, u32[]{:S(2)}) copy-start(f32[2880]{0:T(1024)} %param.19) | copy-start | bytes 34564
  72.7 14.7 %copy-start.5 = (bf16[128,2880]{0,1:T(8,128)(2,1)S(1)}, bf16[128,2880]{0,1:T(8,128)(2,1)}, u32[]{:S(2)}) copy-start(bf16[128,2880]{0,1:T(8,128)(2,1)} %param.13) | copy-start | bytes 2211844
  72.7 14.7 %copy-start.8 = (s32[128,4]{0,1:T(4,128)S(1)}, s32[128,4]{0,1:T(4,128)}, u32[]{:S(2)}) copy-start(s32[128,4]{0,1:T(4,128)} %param.24) | copy-start | bytes 6148
  84.9 62.3 %collective-permute-start.16 = (bf16[728,2880]{1,0:T(8,128)(2,1)S(1)}, bf16[728,2880]{1,0:T(8,128)(2,1)S(1)}, u32[]{:S(2)}, u32[]{:S(2)}) collective-permute-start(bf16[728,2880]{1,0:T(8,128)(2,1)S(1)} %shard_map.128), channel_id=1, source_target_pairs={{0,0},{1,17},{2,2},{3,19},{4,4},{5,21},{6,6},{7,23},{8,8},{9,25},{... | collective-permute-start | bytes 12579848 | tf_op jit(solution)/shard_map/ppermute | solution.py:484
  108.8 7.7 %collective-permute-start.12 = (bf16[64,2880]{1,0:T(8,128)(2,1)S(1)}, bf16[64,2880]{1,0:T(8,128)(2,1)S(1)}, u32[]{:S(2)}, u32[]{:S(2)}) collective-permute-start(bf16[64,2880]{1,0:T(8,128)(2,1)S(1)} %get-tuple-element.152.refs_1_), channel_id=1, source_target_pairs={{16,0},{49,1},{18,2},{51,3},{20,4},{53,5},{22,6},{55,7},{24,8},{57... | collective-permute-start | bytes 1105928 | tf_op jit(solution)/shard_map/ppermute | solution.py:484
  108.9 10.1 %collective-permute-start.10 = (bf16[64,2880]{1,0:T(8,128)(2,1)S(1)}, bf16[64,2880]{1,0:T(8,128)(2,1)S(1)}, u32[]{:S(2)}, u32[]{:S(2)}) collective-permute-start(bf16[64,2880]{1,0:T(8,128)(2,1)S(1)} %get-tuple-element.151.refs_0_), channel_id=1, source_target_pairs={{0,16},{1,49},{2,18},{3,51},{4,20},{5,53},{6,22},{7,55},{8,24},{9,... | collective-permute-start | bytes 1105928 | tf_op jit(solution)/shard_map/ppermute | solution.py:484
  111.6 15.4 %collective-permute-start.14 = (bf16[64,2880]{1,0:T(8,128)(2,1)S(1)}, bf16[64,2880]{1,0:T(8,128)(2,1)S(1)}, u32[]{:S(2)}, u32[]{:S(2)}) collective-permute-start(bf16[64,2880]{1,0:T(8,128)(2,1)S(1)} %get-tuple-element.152.refs_1_), channel_id=1, source_target_pairs={{0,16},{1,49},{2,18},{3,51},{4,20},{5,53},{6,22},{7,55},{8,24},{9,... | collective-permute-start | bytes 1105928 | tf_op jit(solution)/shard_map/ppermute | solution.py:484
  113.0 14.0 %collective-permute-start.15 = (bf16[64,2880]{1,0:T(8,128)(2,1)S(1)}, bf16[64,2880]{1,0:T(8,128)(2,1)S(1)}, u32[]{:S(2)}, u32[]{:S(2)}) collective-permute-start(bf16[64,2880]{1,0:T(8,128)(2,1)S(1)} %get-tuple-element.151.refs_0_), channel_id=1, source_target_pairs={{16,0},{49,1},{18,2},{51,3},{20,4},{53,5},{22,6},{55,7},{24,8},{57... | collective-permute-start | bytes 1105928 | tf_op jit(solution)/shard_map/ppermute | solution.py:484
  116.5 16.4 %collective-permute-start.13 = (bf16[64,2880]{1,0:T(8,128)(2,1)S(1)}, bf16[64,2880]{1,0:T(8,128)(2,1)S(1)}, u32[]{:S(2)}, u32[]{:S(2)}) collective-permute-start(bf16[64,2880]{1,0:T(8,128)(2,1)S(1)} %collective-permute-done.12.refs_3_), channel_id=1, source_target_pairs={{16,0},{49,1},{18,2},{51,3},{20,4},{53,5},{22,6},{55,7},{24,8},{57... | collective-permute-start | bytes 1105928 | tf_op jit(solution)/shard_map/ppermute | solution.py:484
  118.9 16.1 %collective-permute-start.11 = (bf16[64,2880]{1,0:T(8,128)(2,1)S(1)}, bf16[64,2880]{1,0:T(8,128)(2,1)S(1)}, u32[]{:S(2)}, u32[]{:S(2)}) collective-permute-start(bf16[64,2880]{1,0:T(8,128)(2,1)S(1)} %collective-permute-done.10.refs_2_), channel_id=1, source_target_pairs={{0,16},{1,49},{2,18},{3,51},{4,20},{5,53},{6,22},{7,55},{8,24},{9,... | collective-permute-start | bytes 1105928 | tf_op jit(solution)/shard_map/ppermute | solution.py:484
  151.5 7.6 %collective-permute-start.17 = (bf16[64,2880]{1,0:T(8,128)(2,1)S(1)}, bf16[64,2880]{1,0:T(8,128)(2,1)S(1)}, u32[]{:S(2)}, u32[]{:S(2)}) collective-permute-start(bf16[64,2880]{1,0:T(8,128)(2,1)S(1)} %get-tuple-element.149), channel_id=1, source_target_pairs={{0,16},{1,49},{2,18},{3,51},{4,20},{5,53},{6,22},{7,55},{8,24},{9,... | collective-permute-start | bytes 1105928 | tf_op jit(solution)/shard_map/ppermute | solution.py:484
  154.6 7.7 %collective-permute-start.18 = (bf16[64,2880]{1,0:T(8,128)(2,1)S(1)}, bf16[64,2880]{1,0:T(8,128)(2,1)S(1)}, u32[]{:S(2)}, u32[]{:S(2)}) collective-permute-start(bf16[64,2880]{1,0:T(8,128)(2,1)S(1)} %get-tuple-element.150), channel_id=1, source_target_pairs={{16,0},{49,1},{18,2},{51,3},{20,4},{53,5},{22,6},{55,7},{24,8},{57... | collective-permute-start | bytes 1105928 | tf_op jit(solution)/shard_map/ppermute | solution.py:484
  162.4 16.3 %collective-permute-start.20 = (bf16[2,64,2880]{2,1,0:T(8,128)(2,1)S(1)}, bf16[2,64,2880]{2,1,0:T(8,128)(2,1)S(1)}, u32[]{:S(2)}, u32[]{:S(2)}) collective-permute-start(bf16[2,64,2880]{2,1,0:T(8,128)(2,1)S(1)} %pad_maximum_fusion.1), channel_id=1, source_target_pairs={{16,0},{49,1},{18,2},{51,3},{20,4},{53,5},{22,6},{55,7},{24,8},{57... | collective-permute-start | bytes 2211848 | tf_op jit(solution)/shard_map/ppermute | solution.py:484
  162.7 16.0 %collective-permute-start.19 = (bf16[2,64,2880]{2,1,0:T(8,128)(2,1)S(1)}, bf16[2,64,2880]{2,1,0:T(8,128)(2,1)S(1)}, u32[]{:S(2)}, u32[]{:S(2)}) collective-permute-start(bf16[2,64,2880]{2,1,0:T(8,128)(2,1)S(1)} %pad_maximum_fusion), channel_id=1, source_target_pairs={{0,16},{1,49},{2,18},{3,51},{4,20},{5,53},{6,22},{7,55},{8,24},{9,... | collective-permute-start | bytes 2211848 | tf_op jit(solution)/shard_map/ppermute | solution.py:484
  179.0 21.6 %copy-start.9 = (f32[128,4]{0,1:T(4,128)S(1)}, f32[128,4]{0,1:T(4,128)}, u32[]{:S(2)}) copy-start(f32[128,4]{0,1:T(4,128)} %param.25) | copy-start | bytes 6148
where the time goes:
time: 203 us; the launch traced here: 202 us
  waiting for transfers between devices  62.3 us (31%)
  blocking collectives  62.2 us (31%)
  starting transfers between devices  36.7 us (18%)
  Pallas kernels  36.4 us (18%)
  local copies, waits for them, and re-layouts  3.37 us (2%)
    ppermute x16, waiting for transfers between devices, permute(): return lax.ppermute(v, ('ctx', 'exp'), pairs)  46.3 us
    ppermute x16, starting transfers between devices, permute(): return lax.ppermute(v, ('ctx', 'exp'), pairs)  29.2 us
    all_to_all x1, blocking collectives, on_device(): lax.all_to_all(summed, 'exp', split_axis=0, concat_axis=0, tiled=True)  21.5 us
    all_to_all x1, blocking collectives, on_device(): lax.all_to_all(packed, 'ctx', split_axis=0, concat_axis=0, tiled=True, ax...  20.5 us
    all_to_all x1, blocking collectives, on_device(): lax.all_to_all(send, 'exp', split_axis=0, concat_axis=0, tiled=True)  20.2 us
    pallas_call x4, Pallas kernels, experts(): pl.pallas_call(functools.partial(expert_kernel, sizes, near), out_shape=t...  15.5 us
    ppermute x2, waiting for transfers between devices, go_right(): return lax.ppermute(v, 'ctx', RIGHT)  14.2 us
    pallas_call x3, Pallas kernels, attend(): pl.pallas_call(functools.partial(attend_kernel, steps), out_shape=jax.Sha...  12.5 us
  transfers between devices with their start and end apart: 21, of which 14 were waited for; matrix products, arithmetic and copies ran while one was open for 0% of the time, Pallas kernels for 15%

commit v1 on v0

--- a/solution.py
+++ b/solution.py
@@ -220,7 +220,7 @@
             pltpu.VMEM((TOK, 1024), jnp.float32),
             pltpu.VMEM((2, 2 * TOK, 1024), jnp.float32),
         ],
-        compiler_params=params(14),
+        compiler_params=params(11),
         cost_estimate=pl.CostEstimate(
             flops=2 << 30, bytes_accessed=4 << 20, transcendentals=0
         ),
@@ -448,7 +448,7 @@
         scratch_shapes=[pltpu.VMEM((total, D), jnp.bfloat16)]
         + [pltpu.VMEM((FFS, D), jnp.bfloat16)] * (3 if near else 0)
         + [pltpu.SemaphoreType.DMA((len(sizes) + 3,))],
-        compiler_params=params(16 if near else 10),
+        compiler_params=params(13 if near else 8),
         cost_estimate=pl.CostEstimate(
             flops=6 * total * D * FFS, bytes_accessed=4 << 20, transcendentals=0
         ),
@@ -487,32 +487,42 @@
 NEXT = over_all(onward)
 BACK = [(b, a) for a, b in NEXT]
 PARTNER = over_all(partner)
-PARTNER_0 = [(a, b if a % 2 == 0 else a) for a, b in PARTNER]
-PARTNER_1 = [(a, b if a % 2 == 1 else a) for a, b in PARTNER]
+PARTNER_0 = [(a, b) for a, b in PARTNER if a % 2 == 0]
+PARTNER_1 = [(a, b) for a, b in PARTNER if a % 2 == 1]
 ACROSS = over_all(across_y)
 SWAP = over_all(lambda y, x, z, hi, core: (y, x, z, hi, 1 - core))
 
 
+def odd_place(y, x, z, hi, core):
+    return x % 2 == 1 if core == 0 else (x >= 2) == (y == 0)
+
+
+FORWARD = over_all(lambda *at: onward(*at) if odd_place(*at) else onward(*onward(*onward(*at))))
+
+
 def exchange_experts(arrived, own, near):
     half = TOK // 2
+    y, x = lax.axis_index("ctx") // NX, lax.axis_index("ctx") % NX
+    odd = jnp.where(lax.axis_index("exp") % 2 == 0, x % 2 == 1, (x >= 2) == (y == 0))
     own_a, own_b = arrived[:half], arrived[half:]
-    prev_a, next_b = permute(own_a, NEXT), permute(own_b, BACK)
-    prev_b, next_a = permute(own_b, NEXT), permute(own_a, BACK)
-    opp_a, opp_b = permute(prev_a, NEXT), permute(next_b, BACK)
-    early = (own_a, own_b, prev_a, next_b)
+    prev_a, next_a = permute(own_a, NEXT), permute(own_a, BACK)
+    prev_b, next_b = permute(own_b, NEXT), permute(own_b, BACK)
+    opp_a = permute(jnp.where(odd, prev_a, next_a), FORWARD)
+    opp_b = permute(jnp.where(odd, prev_b, next_b), FORWARD)
+    early = (own_a, own_b, prev_a, next_a)
     early_sums = experts(early, own)
-    late = (opp_a, opp_b, prev_b, next_a)
+    late = (opp_a, opp_b, prev_b, next_b)
     late, early_sums = lax.optimization_barrier((late, early_sums))
     late_sums = experts(late, own)
     near, late_sums = lax.optimization_barrier((near, late_sums))
-    far_a, far_b, op_b, on_a = experts(late, near, late_sums)
-    far_a, far_b, op_b, on_a, early, early_sums = lax.optimization_barrier(
-        (far_a, far_b, op_b, on_a, early, early_sums)
+    far_a, far_b, op_b, on_b = experts(late, near, late_sums)
+    far_a, far_b, op_b, on_b, early, early_sums = lax.optimization_barrier(
+        (far_a, far_b, op_b, on_b, early, early_sums)
     )
     far_a, far_b = permute(far_a, NEXT), permute(far_b, BACK)
-    oo_a, oo_b, op_a, on_b = experts(early, near, early_sums)
-    far_a, far_b, oo_a, oo_b, op_a, on_b = lax.optimization_barrier(
-        (far_a, far_b, oo_a, oo_b, op_a, on_b)
+    oo_a, oo_b, op_a, on_a = experts(early, near, early_sums)
+    far_a, far_b, oo_a, oo_b, op_a, on_a = lax.optimization_barrier(
+        (far_a, far_b, oo_a, oo_b, op_a, on_a)
     )
     from_prev = permute(jnp.stack([add(on_a, far_a), on_b]), NEXT)
     from_next = permute(jnp.stack([op_a, add(op_b, far_b)]), BACK)

time: 203 us -> 210 us (1.034)
  waiting for transfers between devices: 62.3 us -> 54.9 us
  Pallas kernels: 36.4 us -> 43.1 us
  starting transfers between devices: 36.7 us -> 42.2 us
    ppermute x2, waiting for transfers between devices: 14.2 us -> 9.18 us  [go_right(): return lax.ppermute(v, 'ctx', RIGHT)]
    pallas_call x4, Pallas kernels: 15.5 us -> 20.4 us  [experts(): pl.pallas_call(functools.partial(expert_kernel, sizes, near), out_shape=t...]
    ppermute x16, starting transfers between devices: 29.2 us -> 33.1 us  [permute(): return lax.ppermute(v, ('ctx', 'exp'), pairs)]
    all_to_all x1, blocking collectives: 20.2 us -> 23.1 us  [on_device(): lax.all_to_all(send, 'exp', split_axis=0, concat_axis=0, tiled=True)]
    ppermute x2, starting transfers between devices: 2.31 us -> 4.5 us  [go_right(): return lax.ppermute(v, 'ctx', RIGHT)]
    all_to_all x1, blocking collectives: 21.5 us -> 19.4 us  [on_device(): lax.all_to_all(summed, 'exp', split_axis=0, concat_axis=0, tiled=True)]
  transfers between devices with their start and end apart: 21 -> 21, of which waited for: 14 -> 13; matrix products, arithmetic and copies ran while one was open for 0% -> 0% of each run, Pallas kernels for 15% -> 18%
where the time goes in v1:
time: 210 us
  blocking collectives  63 us (30%)
  waiting for transfers between devices  54.9 us (26%)
  Pallas kernels  43.1 us (21%)
  starting transfers between devices  42.2 us (20%)
  local copies, waits for them, and re-layouts  5.11 us (2%)
    ppermute x16, waiting for transfers between devices, permute(): return lax.ppermute(v, ('ctx', 'exp'), pairs)  45.7 us
    ppermute x16, starting transfers between devices, permute(): return lax.ppermute(v, ('ctx', 'exp'), pairs)  33.1 us
    all_to_all x1, blocking collectives, on_device(): lax.all_to_all(send, 'exp', split_axis=0, concat_axis=0, tiled=True)  23.1 us
    all_to_all x1, blocking collectives, on_device(): lax.all_to_all(packed, 'ctx', split_axis=0, concat_axis=0, tiled=True, ax...  20.5 us
    pallas_call x4, Pallas kernels, experts(): pl.pallas_call(functools.partial(expert_kernel, sizes, near), out_shape=t...  20.4 us
    all_to_all x1, blocking collectives, on_device(): lax.all_to_all(summed, 'exp', split_axis=0, concat_axis=0, tiled=True)  19.4 us
    pallas_call x3, Pallas kernels, attend(): pl.pallas_call(functools.partial(attend_kernel, steps), out_shape=jax.Sha...  12.3 us
    ppermute x2, waiting for transfers between devices, go_right(): return lax.ppermute(v, 'ctx', RIGHT)  9.18 us
  transfers between devices with their start and end apart: 21, of which 13 were waited for; matrix products, arithmetic and copies ran while one was open for 0% of the time, Pallas kernels for 18%

profile of v1, /device:TPU:1, one launch (start us, length us, event | category | flops | bytes accessed | tf_op | source)
XLA Modules:
  0.0 209.6 jit_solution(8280433933047193664)
XLA Ops:
  0.0 1.6 dynamic-slice_bitcast_fusion
  1.6 0.8 collective-permute-start
  2.4 3.6 %collective-permute-start.2 = (bf16[1440,512]{1,0:T(8,128)(2,1)S(1)}, bf16[1440,512]{1,0:T(8,128)(2,1)S(1)}, u32[]{:S(2)}, u32[]{:S(2)}) collective-permute-start(bf16[1440,512]{1,0:T(8,128)(2,1)S(1)} %dynamic-slice_bitcast_fusion), channel_id=1, source_target_pairs={{0,66},{1,67},{2,64},{3,65},{4,70},{5,71},{6,68},{7,69},{8,74},{9,... | collective-permute-start | bytes 4423688 | tf_op jit(solution)/shard_map/ppermute | solution.py:484
  6.1 0.0 copy-start.2
  6.1 0.2 shard_map.127
  6.3 20.5 %all_to_all.28.pack_ref = bf16[4,144,1280]{2,1,0:T(8,128)(2,1)S(1)} all-to-all(bf16[4,144,1280]{2,1,0:T(8,128)(2,1)S(1)} %shard_map.127), channel_id=1, replica_groups={{0,16,32,48},{64,80,96,112},{1,17,33,49},{65,81,97,113},{2,18,34,50},{6..., dimensions={0} | all-to-all | bytes 2949120 | tf_op jit(solution)/shard_map/all_to_all | solution.py:558
  26.9 1.4 copy-done.5
  28.3 1.3 collective-permute-start.1
  29.6 0.0 copy-start.18
  29.6 2.3 %shard_map.128 = bf16[728,2880]{1,0:T(8,128)(2,1)} custom-call(bf16[360,2880]{1,0:T(8,128)(2,1)S(1)} %bitcast.49, bf16[360,2880]{1,0:T(8,128)(2,1)S(1)} %bitcast.52), custom_call_target="tpu_custom_call" | custom-call | bytes 8388608 | tf_op jit(solution)/shard_map/pallas_call | solution.py:368
  31.9 3.2 %collective-permute-done.2.w_first = bf16[1440,512]{1,0:T(8,128)(2,1)S(1)} collective-permute-done((bf16[1440,512]{1,0:T(8,128)(2,1)S(1)}, bf16[1440,512]{1,0:T(8,128)(2,1)S(1)}, u32[]{:S(2)}, u32[]{:S(2)}) %collective-permute-start.2) | collective-permute-done | bytes 1474592 | tf_op jit(solution)/shard_map/ppermute | solution.py:484
  35.1 0.9 collective-permute-start.9
  36.0 3.1 %collective-permute-start.4 = (bf16[360,2880]{1,0:T(8,128)(2,1)}, bf16[360,2880]{1,0:T(8,128)(2,1)S(1)}, u32[]{:S(2)}, u32[]{:S(2)}) collective-permute-start(bf16[360,2880]{1,0:T(8,128)(2,1)} %bitcast.4.refs_4_), channel_id=1, source_target_pairs={{1,17},{3,19},{5,21},{7,23},{9,25},{11,27},{13,29},{15,31},{17,1},... | collective-permute-start | bytes 6220808 | tf_op jit(solution)/shard_map/ppermute | solution.py:484
  39.2 6.8 %collective-permute-start.3 = (bf16[1440,512]{1,0:T(8,128)(2,1)S(1)}, bf16[1440,512]{1,0:T(8,128)(2,1)S(1)}, u32[]{:S(2)}, u32[]{:S(2)}) collective-permute-start(bf16[1440,512]{1,0:T(8,128)(2,1)S(1)} %collective-permute-done.2.w_first), channel_id=1, source_target_pairs={{0,1},{1,0},{2,3},{3,2},{4,5},{5,4},{6,7},{7,6},{8,9},{9,8},{10,11... | collective-permute-start | bytes 4423688 | tf_op jit(solution)/shard_map/ppermute | solution.py:484
  46.0 3.5 %shard_map.129.attn = bf16[128,1024]{1,0:T(8,128)(2,1)S(1)} custom-call(f32[64]{0:T(128)S(1)} %copy-done.18, bf16[4,144,1280]{2,1,0:T(8,128)(2,1)S(1)} %all_to_all.28.pack_ref, bf16[4,144,256]{2,1,0:T(8,128)(2,1)S(1)} %collective-permute-done.1.low_ref), custom_call_target="tpu_custom_call" | custom-call | flops 2147483648 | bytes 4194304 | tf_op jit(solution)/shard_map/pallas_call | solution.py:209
  49.5 1.7 shard_map.130
  51.2 2.1 collective-permute-start.5
  53.2 1.7 collective-permute-start.6
  55.0 5.8 %shard_map.131.attn = bf16[256,1024]{1,0:T(8,128)(2,1)S(1)} custom-call(f32[64]{0:T(128)S(1)} %copy-done.18, bf16[4,144,1280]{2,1,0:T(8,128)(2,1)S(1)} %all_to_all.28.pack_ref, bf16[4,144,256]{2,1,0:T(8,128)(2,1)S(1)} %collective-permute-done.1.low_ref), custom_call_target="tpu_custom_call" | custom-call | flops 2147483648 | bytes 4194304 | tf_op jit(solution)/shard_map/pallas_call | solution.py:209
  60.7 6.8 %collective-permute-done.4.refs_5_ = bf16[360,2880]{1,0:T(8,128)(2,1)S(1)} collective-permute-done((bf16[360,2880]{1,0:T(8,128)(2,1)}, bf16[360,2880]{1,0:T(8,128)(2,1)S(1)}, u32[]{:S(2)}, u32[]{:S(2)}) %collective-permute-start.4) | collective-permute-done | bytes 2073632 | tf_op jit(solution)/shard_map/ppermute | solution.py:484
  67.5 4.3 %collective-permute-done.5.refs_0_ = bf16[1440,128]{1,0:T(8,128)(2,1)S(1)} collective-permute-done((bf16[1440,128]{1,0:T(8,128)(2,1)S(1)}, bf16[1440,128]{1,0:T(8,128)(2,1)S(1)}, u32[]{:S(2)}, u32[]{:S(2)}) %collective-permute-start.5) | collective-permute-done | bytes 368672 | tf_op jit(solution)/shard_map/ppermute | solution.py:41
  71.8 1.7 shard_map.132
  73.6 2.5 %collective-permute-start.7 = (bf16[2880,128]{1,0:T(8,128)(2,1)S(1)}, bf16[2880,128]{1,0:T(8,128)(2,1)S(1)}, u32[]{:S(2)}, u32[]{:S(2)}) collective-permute-start(bf16[2880,128]{1,0:T(8,128)(2,1)S(1)} %get-tuple-element.103), channel_id=1, source_target_pairs={{0,16},{16,32},{32,48},{48,0},{64,80},{80,96},{96,112},{112,64},{1... | collective-permute-start | bytes 2211848 | tf_op jit(solution)/shard_map/ppermute | solution.py:41
  76.0 1.6 collective-permute-start.8
  77.6 3.0 %shard_map.133.attn = bf16[128,1024]{1,0:T(8,128)(2,1)S(1)} custom-call(f32[64]{0:T(128)S(1)} %copy-done.18, bf16[4,144,1280]{2,1,0:T(8,128)(2,1)S(1)} %all_to_all.28.pack_ref, bf16[4,144,256]{2,1,0:T(8,128)(2,1)S(1)} %collective-permute-done.1.low_ref), custom_call_target="tpu_custom_call" | custom-call | flops 2147483648 | bytes 4194304 | tf_op jit(solution)/shard_map/pallas_call | solution.py:209
  80.6 0.0 copy-start.19
  80.6 0.0 copy-start.12
  80.7 1.7 shard_map.134
  82.4 4.9 %collective-permute-done.7.left = bf16[2880,128]{1,0:T(8,128)(2,1)S(1)} collective-permute-done((bf16[2880,128]{1,0:T(8,128)(2,1)S(1)}, bf16[2880,128]{1,0:T(8,128)(2,1)S(1)}, u32[]{:S(2)}, u32[]{:S(2)}) %collective-permute-start.7) | collective-permute-done | bytes 737312 | tf_op jit(solution)/shard_map/ppermute | solution.py:41
  87.3 0.1 collective-permute-done.8.right
  87.4 3.5 %collective-permute-start.16 = (bf16[728,2880]{1,0:T(8,128)(2,1)}, bf16[728,2880]{1,0:T(8,128)(2,1)}, u32[]{:S(2)}, u32[]{:S(2)}) collective-permute-start(bf16[728,2880]{1,0:T(8,128)(2,1)} %shard_map.128), channel_id=1, source_target_pairs={{1,17},{3,19},{5,21},{7,23},{9,25},{11,27},{13,29},{15,31},{17,1},... | collective-permute-start | bytes 12579848 | tf_op jit(solution)/shard_map/ppermute | solution.py:484
  90.9 1.1 shard_map.135
  92.1 23.1 %all_to_all.29 = bf16[16,8,2880]{2,1,0:T(8,128)(2,1)S(1)} all-to-all(bf16[16,8,2880]{2,1,0:T(8,128)(2,1)S(1)} %bitcast.58), channel_id=1, replica_groups=mesh['ctx'=8,'exp'=16] {'exp'}, dimensions={0} | all-to-all | bytes 1474560 | tf_op jit(solution)/shard_map/all_to_all | solution.py:591
  115.2 2.0 copy-done.4
  117.2 0.1 fusion.4
  117.2 0.3 collective-permute-start.14
  117.6 2.4 %collective-permute-start.13 = (bf16[64,2880]{1,0:T(8,128)(2,1)S(1)}, bf16[64,2880]{1,0:T(8,128)(2,1)}, u32[]{:S(2)}, u32[]{:S(2)}) collective-permute-start(bf16[64,2880]{1,0:T(8,128)(2,1)S(1)} %get-tuple-element.152.refs_1_), channel_id=1, source_target_pairs={{0,16},{1,49},{2,18},{3,51},{4,20},{5,53},{6,22},{7,55},{8,24},{9,... | collective-permute-start | bytes 1105928 | tf_op jit(solution)/shard_map/ppermute | solution.py:484
  120.0 2.7 %collective-permute-start.10 = (bf16[64,2880]{1,0:T(8,128)(2,1)S(1)}, bf16[64,2880]{1,0:T(8,128)(2,1)S(1)}, u32[]{:S(2)}, u32[]{:S(2)}) collective-permute-start(bf16[64,2880]{1,0:T(8,128)(2,1)S(1)} %get-tuple-element.151.refs_0_), channel_id=1, source_target_pairs={{0,16},{1,49},{2,18},{3,51},{4,20},{5,53},{6,22},{7,55},{8,24},{9,... | collective-permute-start | bytes 1105928 | tf_op jit(solution)/shard_map/ppermute | solution.py:484
  122.7 4.0 %collective-permute-done.14.refs_3_ = bf16[64,2880]{1,0:T(8,128)(2,1)S(1)} collective-permute-done((bf16[64,2880]{1,0:T(8,128)(2,1)S(1)}, bf16[64,2880]{1,0:T(8,128)(2,1)S(1)}, u32[]{:S(2)}, u32[]{:S(2)}) %collective-permute-start.14) | collective-permute-done | bytes 368672 | tf_op jit(solution)/shard_map/ppermute | solution.py:484
  126.7 1.9 collective-permute-done.13.refs_2_
  128.6 0.1 broadcast_select_fusion
  128.6 1.7 collective-permute-start.15
  130.4 4.3 %collective-permute-done.11.refs_3_ = bf16[64,2880]{1,0:T(8,128)(2,1)S(1)} collective-permute-done((bf16[64,2880]{1,0:T(8,128)(2,1)S(1)}, bf16[64,2880]{1,0:T(8,128)(2,1)S(1)}, u32[]{:S(2)}, u32[]{:S(2)}) %collective-permute-start.11) | collective-permute-done | bytes 368672 | tf_op jit(solution)/shard_map/ppermute | solution.py:484
  134.7 2.0 collective-permute-done.10.refs_2_
  136.7 0.9 collective-permute-start.12
  137.6 5.2 %shard_map.136 = (bf16[64,2880]{1,0:T(8,128)(2,1)S(1)}, bf16[64,2880]{1,0:T(8,128)(2,1)S(1)}, bf16[64,2880]{1,0:T(8,128)(2,1)S(1)}, bf16[64,2880]{1,0:T(8,128)(2,1)S(1)}) custom-call(bf16[64,2880]{1,0:T(8,128)(2,1)S(1)} %get-tuple-element.151.refs_0_, bf16[64,2880]{1,0:T(8,128)(2,1)S(1)} %get-tuple-element.152.refs_1_, ...), custom_call_target="tpu_custom_call" | custom-call | flops 1592524800 | bytes 4194304 | tf_op jit(solution)/shard_map/pallas_call | solution.py:441
  142.7 1.0 collective-permute-done.12.refs_0_
  143.7 6.3 %shard_map.137 = (bf16[64,2880]{1,0:T(8,128)(2,1)S(1)}, bf16[64,2880]{1,0:T(8,128)(2,1)S(1)}, bf16[64,2880]{1,0:T(8,128)(2,1)S(1)}, bf16[64,2880]{1,0:T(8,128)(2,1)S(1)}) custom-call(bf16[64,2880]{1,0:T(8,128)(2,1)S(1)} %collective-permute-done.12.refs_0_, bf16[64,2880]{1,0:T(8,128)(2,1)S(1)} %collective-permute-done.15.refs_1_, ...), custom_call_target="tpu_custom_call" | custom-call | flops 1592524800 | bytes 4194304 | tf_op jit(solution)/shard_map/pallas_call | solution.py:441
  150.1 4.5 %shard_map.138 = (bf16[64,2880]{1,0:T(8,128)(2,1)S(1)}, bf16[64,2880]{1,0:T(8,128)(2,1)S(1)}, bf16[64,2880]{1,0:T(8,128)(2,1)S(1)}, bf16[64,2880]{1,0:T(8,128)(2,1)S(1)}) custom-call(bf16[64,2880]{1,0:T(8,128)(2,1)S(1)} %collective-permute-done.12.refs_0_, bf16[64,2880]{1,0:T(8,128)(2,1)S(1)} %collective-permute-done.15.refs_1_, ...), custom_call_target="tpu_custom_call" | custom-call | flops 1592524800 | bytes 4194304 | tf_op jit(solution)/shard_map/pallas_call | solution.py:441
  154.6 3.5 %collective-permute-start.17 = (bf16[64,2880]{1,0:T(8,128)(2,1)S(1)}, bf16[64,2880]{1,0:T(8,128)(2,1)S(1)}, u32[]{:S(2)}, u32[]{:S(2)}) collective-permute-start(bf16[64,2880]{1,0:T(8,128)(2,1)S(1)} %get-tuple-element.149), channel_id=1, source_target_pairs={{0,16},{1,49},{2,18},{3,51},{4,20},{5,53},{6,22},{7,55},{8,24},{9,... | collective-permute-start | bytes 1105928 | tf_op jit(solution)/shard_map/ppermute | solution.py:484
  158.0 4.5 %shard_map.139 = (bf16[64,2880]{1,0:T(8,128)(2,1)S(1)}, bf16[64,2880]{1,0:T(8,128)(2,1)S(1)}, bf16[64,2880]{1,0:T(8,128)(2,1)S(1)}, bf16[64,2880]{1,0:T(8,128)(2,1)S(1)}) custom-call(bf16[64,2880]{1,0:T(8,128)(2,1)S(1)} %get-tuple-element.151.refs_0_, bf16[64,2880]{1,0:T(8,128)(2,1)S(1)} %get-tuple-element.152.refs_1_, ...), custom_call_target="tpu_custom_call" | custom-call | flops 1592524800 | bytes 4194304 | tf_op jit(solution)/shard_map/pallas_call | solution.py:441
  162.5 0.6 collective-permute-done.17
  163.2 6.5 %collective-permute-done.18 = bf16[64,2880]{1,0:T(8,128)(2,1)S(1)} collective-permute-done((bf16[64,2880]{1,0:T(8,128)(2,1)S(1)}, bf16[64,2880]{1,0:T(8,128)(2,1)S(1)}, u32[]{:S(2)}, u32[]{:S(2)}) %collective-permute-start.18) | collective-permute-done | bytes 368672 | tf_op jit(solution)/shard_map/ppermute | solution.py:484
  169.7 0.1 fusion.3
  169.8 0.1 pad_maximum_fusion.1
  169.9 0.1 collective-permute-start.20
  170.0 0.1 fusion.2
  170.1 0.1 pad_maximum_fusion
  170.1 2.7 %collective-permute-start.19 = (bf16[2,64,2880]{2,1,0:T(8,128)(2,1)S(1)}, bf16[2,64,2880]{2,1,0:T(8,128)(2,1)S(1)}, u32[]{:S(2)}, u32[]{:S(2)}) collective-permute-start(bf16[2,64,2880]{2,1,0:T(8,128)(2,1)S(1)} %pad_maximum_fusion), channel_id=1, source_target_pairs={{0,16},{1,49},{2,18},{3,51},{4,20},{5,53},{6,22},{7,55},{8,24},{9,... | collective-permute-start | bytes 2211848 | tf_op jit(solution)/shard_map/ppermute | solution.py:484
  172.9 15.3 %collective-permute-done.20 = bf16[2,64,2880]{2,1,0:T(8,128)(2,1)S(1)} collective-permute-done((bf16[2,64,2880]{2,1,0:T(8,128)(2,1)S(1)}, bf16[2,64,2880]{2,1,0:T(8,128)(2,1)S(1)}, u32[]{:S(2)}, u32[]{:S(2)}) %collective-permute-start.20) | collective-permute-done | bytes 737312 | tf_op jit(solution)/shard_map/ppermute | solution.py:484
  188.2 0.3 fusion.1
  188.6 0.1 maximum_bitcast_fusion
  188.6 19.4 %all_to_all.30 = bf16[16,8,2880]{2,1,0:T(8,128)(2,1)S(1)} all-to-all(bf16[16,8,2880]{2,1,0:T(8,128)(2,1)S(1)} %maximum_bitcast_fusion), channel_id=1, replica_groups=mesh['ctx'=8,'exp'=16] {'exp'}, dimensions={0} | all-to-all | bytes 1474560 | tf_op jit(solution)/shard_map/all_to_all | solution.py:594
  208.0 1.6 shard_map.140
  (52 shorter events, 0.2 us)
Async XLA Ops:
  0.0 6.1 %copy-start.17 = (s32[128]{0:T(128)S(1)}, s32[128]{0:T(128)}, u32[]{:S(2)}) copy-start(s32[128]{0:T(128)} %param.18) | copy-start | bytes 1540
  0.0 6.1 %copy-start.14 = (bf16[128,512]{1,0:T(8,128)(2,1)S(1)}, bf16[128,512]{1,0:T(8,128)(2,1)}, u32[]{:S(2)}) copy-start(bf16[128,512]{1,0:T(8,128)(2,1)} %v_ref.1) | copy-start | bytes 393220
  0.0 6.1 %copy-start.13 = (bf16[128,512]{1,0:T(8,128)(2,1)S(1)}, bf16[128,512]{1,0:T(8,128)(2,1)}, u32[]{:S(2)}) copy-start(bf16[128,512]{1,0:T(8,128)(2,1)} %k_ref.1) | copy-start | bytes 393220
  0.0 6.1 %copy-start.11 = (bf16[128,4096]{1,0:T(8,128)(2,1)S(1)}, bf16[128,4096]{1,0:T(8,128)(2,1)}, u32[]{:S(2)}) copy-start(bf16[128,4096]{1,0:T(8,128)(2,1)} %q_ref.1) | copy-start | bytes 3145732
  1.6 25.3 %collective-permute-start = (bf16[360,2880]{1,0:T(8,128)(2,1)}, bf16[360,2880]{1,0:T(8,128)(2,1)S(1)}, u32[]{:S(2)}, u32[]{:S(2)}) collective-permute-start(bf16[360,2880]{1,0:T(8,128)(2,1)} %bitcast.4.refs_4_), channel_id=1, source_target_pairs={{0,64},{2,66},{4,68},{6,70},{8,72},{10,74},{12,76},{14,78},{16,80}... | collective-permute-start | bytes 6220808 | tf_op jit(solution)/shard_map/ppermute | solution.py:484
  2.4 32.7 %collective-permute-start.2 = (bf16[1440,512]{1,0:T(8,128)(2,1)S(1)}, bf16[1440,512]{1,0:T(8,128)(2,1)S(1)}, u32[]{:S(2)}, u32[]{:S(2)}) collective-permute-start(bf16[1440,512]{1,0:T(8,128)(2,1)S(1)} %dynamic-slice_bitcast_fusion), channel_id=1, source_target_pairs={{0,66},{1,67},{2,64},{3,65},{4,70},{5,71},{6,68},{7,69},{8,74},{9,... | collective-permute-start | bytes 4423688 | tf_op jit(solution)/shard_map/ppermute | solution.py:484
  6.1 23.5 %copy-start.2 = (bf16[1,360,2880]{2,1,0:T(8,128)(2,1)S(1)}, bf16[1,360,2880]{2,1,0:T(8,128)(2,1)}, u32[]{:S(2)}) copy-start(bf16[1,360,2880]{2,1,0:T(8,128)(2,1)} %param.23) | copy-start | bytes 6220804
  6.3 23.3 %copy-start.1 = (bf16[1,2880,360]{1,2,0:T(8,128)(2,1)S(1)}, bf16[1,2880,360]{1,2,0:T(8,128)(2,1)}, u32[]{:S(2)}) copy-start(bf16[1,2880,360]{1,2,0:T(8,128)(2,1)} %param.22) | copy-start | bytes 6220804
  26.9 1.4 copy-start.5
  28.3 6.9 %collective-permute-start.1 = (bf16[4,144,256]{2,1,0:T(8,128)(2,1)S(1)}, bf16[4,144,256]{2,1,0:T(8,128)(2,1)S(1)}, u32[]{:S(2)}, u32[]{:S(2)}) collective-permute-start(bf16[4,144,256]{2,1,0:T(8,128)(2,1)S(1)} %slice.21), channel_id=1, source_target_pairs={{0,64},{16,80},{32,96},{48,112},{1,65},{17,81},{33,97},{49,113},{2... | collective-permute-start | bytes 884744 | tf_op jit(solution)/shard_map/ppermute | solution.py:567
  29.6 16.4 %copy-start.18 = (f32[64]{0:T(128)S(1)}, f32[64]{0:T(128)}, u32[]{:S(2)}) copy-start(f32[64]{0:T(128)} %sinks.5) | copy-start | bytes 772
  31.9 17.6 %copy-start = (bf16[512,2880]{0,1:T(8,128)(2,1)S(1)}, bf16[512,2880]{0,1:T(8,128)(2,1)}, u32[]{:S(2)}) copy-start(bf16[512,2880]{0,1:T(8,128)(2,1)} %param.20) | copy-start | bytes 8847364
  35.1 80.1 %collective-permute-start.9 = (bf16[728,2880]{1,0:T(8,128)(2,1)}, bf16[728,2880]{1,0:T(8,128)(2,1)S(1)}, u32[]{:S(2)}, u32[]{:S(2)}) collective-permute-start(bf16[728,2880]{1,0:T(8,128)(2,1)} %shard_map.128), channel_id=1, source_target_pairs={{0,64},{2,66},{4,68},{6,70},{8,72},{10,74},{12,76},{14,78},{16,80}... | collective-permute-start | bytes 12579848 | tf_op jit(solution)/shard_map/ppermute | solution.py:484
  36.0 31.5 %collective-permute-start.4 = (bf16[360,2880]{1,0:T(8,128)(2,1)}, bf16[360,2880]{1,0:T(8,128)(2,1)S(1)}, u32[]{:S(2)}, u32[]{:S(2)}) collective-permute-start(bf16[360,2880]{1,0:T(8,128)(2,1)} %bitcast.4.refs_4_), channel_id=1, source_target_pairs={{1,17},{3,19},{5,21},{7,23},{9,25},{11,27},{13,29},{15,31},{17,1},... | collective-permute-start | bytes 6220808 | tf_op jit(solution)/shard_map/ppermute | solution.py:484
  39.2 10.3 %collective-permute-start.3 = (bf16[1440,512]{1,0:T(8,128)(2,1)S(1)}, bf16[1440,512]{1,0:T(8,128)(2,1)S(1)}, u32[]{:S(2)}, u32[]{:S(2)}) collective-permute-start(bf16[1440,512]{1,0:T(8,128)(2,1)S(1)} %collective-permute-done.2.w_first), channel_id=1, source_target_pairs={{0,1},{1,0},{2,3},{3,2},{4,5},{5,4},{6,7},{7,6},{8,9},{9,8},{10,11... | collective-permute-start | bytes 4423688 | tf_op jit(solution)/shard_map/ppermute | solution.py:484
  51.2 20.6 %collective-permute-start.5 = (bf16[1440,128]{1,0:T(8,128)(2,1)S(1)}, bf16[1440,128]{1,0:T(8,128)(2,1)S(1)}, u32[]{:S(2)}, u32[]{:S(2)}) collective-permute-start(bf16[1440,128]{1,0:T(8,128)(2,1)S(1)} %get-tuple-element.99), channel_id=1, source_target_pairs={{0,16},{16,32},{32,48},{48,0},{64,80},{80,96},{96,112},{112,64},{1... | collective-permute-start | bytes 1105928 | tf_op jit(solution)/shard_map/ppermute | solution.py:41
  53.2 18.6 %collective-permute-start.6 = (bf16[1440,128]{1,0:T(8,128)(2,1)S(1)}, bf16[1440,128]{1,0:T(8,128)(2,1)S(1)}, u32[]{:S(2)}, u32[]{:S(2)}) collective-permute-start(bf16[1440,128]{1,0:T(8,128)(2,1)S(1)} %get-tuple-element.100), channel_id=1, source_target_pairs={{0,48},{16,0},{32,16},{48,32},{64,112},{80,64},{96,80},{112,96},{1... | collective-permute-start | bytes 1105928 | tf_op jit(solution)/shard_map/ppermute | solution.py:45
  67.5 6.0 %copy-start.7 = (bf16[360,2880]{1,0:T(8,128)(2,1)}, bf16[360,2880]{1,0:T(8,128)(2,1)S(1)}, u32[]{:S(2)}) copy-start(bf16[360,2880]{1,0:T(8,128)(2,1)S(1)} %collective-permute-done.4.refs_5_) | copy-start | bytes 6220804
  73.6 13.7 %collective-permute-start.7 = (bf16[2880,128]{1,0:T(8,128)(2,1)S(1)}, bf16[2880,128]{1,0:T(8,128)(2,1)S(1)}, u32[]{:S(2)}, u32[]{:S(2)}) collective-permute-start(bf16[2880,128]{1,0:T(8,128)(2,1)S(1)} %get-tuple-element.103), channel_id=1, source_target_pairs={{0,16},{16,32},{32,48},{48,0},{64,80},{80,96},{96,112},{112,64},{1... | collective-permute-start | bytes 2211848 | tf_op jit(solution)/shard_map/ppermute | solution.py:41
  76.0 11.3 %collective-permute-start.8 = (bf16[2880,128]{1,0:T(8,128)(2,1)S(1)}, bf16[2880,128]{1,0:T(8,128)(2,1)S(1)}, u32[]{:S(2)}, u32[]{:S(2)}) collective-permute-start(bf16[2880,128]{1,0:T(8,128)(2,1)S(1)} %get-tuple-element.104), channel_id=1, source_target_pairs={{0,48},{16,0},{32,16},{48,32},{64,112},{80,64},{96,80},{112,96},{1... | collective-permute-start | bytes 2211848 | tf_op jit(solution)/shard_map/ppermute | solution.py:45
  80.6 10.3 %copy-start.19 = (f32[2880]{0:T(1024)S(1)}, f32[2880]{0:T(1024)}, u32[]{:S(2)}) copy-start(f32[2880]{0:T(1024)} %param.19) | copy-start | bytes 34564
  80.6 10.3 %copy-start.12 = (bf16[128,2880]{0,1:T(8,128)(2,1)S(1)}, bf16[128,2880]{0,1:T(8,128)(2,1)}, u32[]{:S(2)}) copy-start(bf16[128,2880]{0,1:T(8,128)(2,1)} %param.13) | copy-start | bytes 2211844
  80.7 10.3 %copy-start.15 = (s32[128,4]{0,1:T(4,128)S(1)}, s32[128,4]{0,1:T(4,128)}, u32[]{:S(2)}) copy-start(s32[128,4]{0,1:T(4,128)} %param.24) | copy-start | bytes 6148
  87.4 62.6 %collective-permute-start.16 = (bf16[728,2880]{1,0:T(8,128)(2,1)}, bf16[728,2880]{1,0:T(8,128)(2,1)}, u32[]{:S(2)}, u32[]{:S(2)}) collective-permute-start(bf16[728,2880]{1,0:T(8,128)(2,1)} %shard_map.128), channel_id=1, source_target_pairs={{1,17},{3,19},{5,21},{7,23},{9,25},{11,27},{13,29},{15,31},{17,1},... | collective-permute-start | bytes 12579848 | tf_op jit(solution)/shard_map/ppermute | solution.py:484
  92.1 23.1 %copy-start.9 = (f32[2880,128]{1,0:T(8,128)}, f32[2880,128]{1,0:T(8,128)S(1)}, u32[]{:S(2)}) copy-start(f32[2880,128]{1,0:T(8,128)S(1)} %get-tuple-element.114.hidden) | copy-start | bytes 4423684
  115.2 2.0 copy-start.4
  117.2 9.5 %collective-permute-start.14 = (bf16[64,2880]{1,0:T(8,128)(2,1)S(1)}, bf16[64,2880]{1,0:T(8,128)(2,1)S(1)}, u32[]{:S(2)}, u32[]{:S(2)}) collective-permute-start(bf16[64,2880]{1,0:T(8,128)(2,1)S(1)} %get-tuple-element.152.refs_1_), channel_id=1, source_target_pairs={{16,0},{49,1},{18,2},{51,3},{20,4},{53,5},{22,6},{55,7},{24,8},{57... | collective-permute-start | bytes 1105928 | tf_op jit(solution)/shard_map/ppermute | solution.py:484
  117.6 11.0 %collective-permute-start.13 = (bf16[64,2880]{1,0:T(8,128)(2,1)S(1)}, bf16[64,2880]{1,0:T(8,128)(2,1)}, u32[]{:S(2)}, u32[]{:S(2)}) collective-permute-start(bf16[64,2880]{1,0:T(8,128)(2,1)S(1)} %get-tuple-element.152.refs_1_), channel_id=1, source_target_pairs={{0,16},{1,49},{2,18},{3,51},{4,20},{5,53},{6,22},{7,55},{8,24},{9,... | collective-permute-start | bytes 1105928 | tf_op jit(solution)/shard_map/ppermute | solution.py:484
  120.0 17.6 %copy-start.3 = (bf16[1,360,2880]{2,1,0:T(8,128)(2,1)S(1)}, bf16[1,360,2880]{2,1,0:T(8,128)(2,1)}, u32[]{:S(2)}) copy-start(bf16[1,360,2880]{2,1,0:T(8,128)(2,1)} %param.23) | copy-start | bytes 6220804
  120.0 14.7 %collective-permute-start.11 = (bf16[64,2880]{1,0:T(8,128)(2,1)S(1)}, bf16[64,2880]{1,0:T(8,128)(2,1)S(1)}, u32[]{:S(2)}, u32[]{:S(2)}) collective-permute-start(bf16[64,2880]{1,0:T(8,128)(2,1)S(1)} %get-tuple-element.151.refs_0_), channel_id=1, source_target_pairs={{16,0},{49,1},{18,2},{51,3},{20,4},{53,5},{22,6},{55,7},{24,8},{57... | collective-permute-start | bytes 1105928 | tf_op jit(solution)/shard_map/ppermute | solution.py:484
  120.0 16.6 %collective-permute-start.10 = (bf16[64,2880]{1,0:T(8,128)(2,1)S(1)}, bf16[64,2880]{1,0:T(8,128)(2,1)S(1)}, u32[]{:S(2)}, u32[]{:S(2)}) collective-permute-start(bf16[64,2880]{1,0:T(8,128)(2,1)S(1)} %get-tuple-element.151.refs_0_), channel_id=1, source_target_pairs={{0,16},{1,49},{2,18},{3,51},{4,20},{5,53},{6,22},{7,55},{8,24},{9,... | collective-permute-start | bytes 1105928 | tf_op jit(solution)/shard_map/ppermute | solution.py:484
  128.6 14.1 %collective-permute-start.15 = (bf16[64,2880]{1,0:T(8,128)(2,1)S(1)}, bf16[64,2880]{1,0:T(8,128)(2,1)S(1)}, u32[]{:S(2)}, u32[]{:S(2)}) collective-permute-start(bf16[64,2880]{1,0:T(8,128)(2,1)S(1)} %broadcast_select_fusion), channel_id=1, source_target_pairs={{0,48},{1,65},{2,50},{3,67},{4,52},{5,69},{6,54},{7,71},{8,56},{9,... | collective-permute-start | bytes 1105928 | tf_op jit(solution)/shard_map/ppermute | solution.py:484
  136.7 7.0 %collective-permute-start.12 = (bf16[64,2880]{1,0:T(8,128)(2,1)S(1)}, bf16[64,2880]{1,0:T(8,128)(2,1)S(1)}, u32[]{:S(2)}, u32[]{:S(2)}) collective-permute-start(bf16[64,2880]{1,0:T(8,128)(2,1)S(1)} %broadcast_select_fusion.1), channel_id=1, source_target_pairs={{0,48},{1,65},{2,50},{3,67},{4,52},{5,69},{6,54},{7,71},{8,56},{9,... | collective-permute-start | bytes 1105928 | tf_op jit(solution)/shard_map/ppermute | solution.py:484
  137.6 12.5 %copy-start.8 = (bf16[360,2880]{1,0:T(8,128)(2,1)S(1)}, bf16[360,2880]{1,0:T(8,128)(2,1)}, u32[]{:S(2)}) copy-start(bf16[360,2880]{1,0:T(8,128)(2,1)} %copy-done.7) | copy-start | bytes 6220804
  143.7 6.3 %slice-start = ((s8[4286464]{0:T(1024)(128)(4,1)}), s8[4194304]{0:T(1024)(128)(4,1)S(1)}, s32[]{:S(2)}) async-start(s8[4286464]{0:T(1024)(128)(4,1)} %bitcast.55), calls=%async_computation.3 | async-start | bytes 8388608
  143.7 6.3 %slice-start.1 = ((s8[4286464]{0:T(1024)(128)(4,1)}), s8[92160]{0:T(1024)(128)(4,1)S(1)}, s32[]{:S(2)}) async-start(s8[4286464]{0:T(1024)(128)(4,1)} %bitcast.55), calls=%async_computation.4 | async-start | bytes 184320
  143.7 6.3 %copy-start.6 = (bf16[360,2880]{1,0:T(8,128)(2,1)S(1)}, bf16[360,2880]{1,0:T(8,128)(2,1)}, u32[]{:S(2)}) copy-start(bf16[360,2880]{1,0:T(8,128)(2,1)} %copy-done.5) | copy-start | bytes 6220804
  154.6 8.6 %collective-permute-start.17 = (bf16[64,2880]{1,0:T(8,128)(2,1)S(1)}, bf16[64,2880]{1,0:T(8,128)(2,1)S(1)}, u32[]{:S(2)}, u32[]{:S(2)}) collective-permute-start(bf16[64,2880]{1,0:T(8,128)(2,1)S(1)} %get-tuple-element.149), channel_id=1, source_target_pairs={{0,16},{1,49},{2,18},{3,51},{4,20},{5,53},{6,22},{7,55},{8,24},{9,... | collective-permute-start | bytes 1105928 | tf_op jit(solution)/shard_map/ppermute | solution.py:484
  158.0 11.6 %collective-permute-start.18 = (bf16[64,2880]{1,0:T(8,128)(2,1)S(1)}, bf16[64,2880]{1,0:T(8,128)(2,1)S(1)}, u32[]{:S(2)}, u32[]{:S(2)}) collective-permute-start(bf16[64,2880]{1,0:T(8,128)(2,1)S(1)} %get-tuple-element.150), channel_id=1, source_target_pairs={{16,0},{49,1},{18,2},{51,3},{20,4},{53,5},{22,6},{55,7},{24,8},{57... | collective-permute-start | bytes 1105928 | tf_op jit(solution)/shard_map/ppermute | solution.py:484
  169.9 18.3 %collective-permute-start.20 = (bf16[2,64,2880]{2,1,0:T(8,128)(2,1)S(1)}, bf16[2,64,2880]{2,1,0:T(8,128)(2,1)S(1)}, u32[]{:S(2)}, u32[]{:S(2)}) collective-permute-start(bf16[2,64,2880]{2,1,0:T(8,128)(2,1)S(1)} %pad_maximum_fusion.1), channel_id=1, source_target_pairs={{16,0},{49,1},{18,2},{51,3},{20,4},{53,5},{22,6},{55,7},{24,8},{57... | collective-permute-start | bytes 2211848 | tf_op jit(solution)/shard_map/ppermute | solution.py:484
  170.1 18.1 %collective-permute-start.19 = (bf16[2,64,2880]{2,1,0:T(8,128)(2,1)S(1)}, bf16[2,64,2880]{2,1,0:T(8,128)(2,1)S(1)}, u32[]{:S(2)}, u32[]{:S(2)}) collective-permute-start(bf16[2,64,2880]{2,1,0:T(8,128)(2,1)S(1)} %pad_maximum_fusion), channel_id=1, source_target_pairs={{0,16},{1,49},{2,18},{3,51},{4,20},{5,53},{6,22},{7,55},{8,24},{9,... | collective-permute-start | bytes 2211848 | tf_op jit(solution)/shard_map/ppermute | solution.py:484
  188.5 19.5 %copy-start.10 = (f32[2880,128]{1,0:T(8,128)S(1)}, f32[2880,128]{1,0:T(8,128)}, u32[]{:S(2)}) copy-start(f32[2880,128]{1,0:T(8,128)} %copy-done.9) | copy-start | bytes 4423684
  188.5 19.5 %copy-start.16 = (f32[128,4]{0,1:T(4,128)S(1)}, f32[128,4]{0,1:T(4,128)}, u32[]{:S(2)}) copy-start(f32[128,4]{0,1:T(4,128)} %param.25) | copy-start | bytes 6148

commit v2 on v0

--- a/solution.py
+++ b/solution.py
@@ -448,7 +448,7 @@
         scratch_shapes=[pltpu.VMEM((total, D), jnp.bfloat16)]
         + [pltpu.VMEM((FFS, D), jnp.bfloat16)] * (3 if near else 0)
         + [pltpu.SemaphoreType.DMA((len(sizes) + 3,))],
-        compiler_params=params(16 if near else 10),
+        compiler_params=params(16),
         cost_estimate=pl.CostEstimate(
             flops=6 * total * D * FFS, bytes_accessed=4 << 20, transcendentals=0
         ),
@@ -487,8 +487,8 @@
 NEXT = over_all(onward)
 BACK = [(b, a) for a, b in NEXT]
 PARTNER = over_all(partner)
-PARTNER_0 = [(a, b if a % 2 == 0 else a) for a, b in PARTNER]
-PARTNER_1 = [(a, b if a % 2 == 1 else a) for a, b in PARTNER]
+PARTNER_0 = [(a, b) for a, b in PARTNER if a % 2 == 0]
+PARTNER_1 = [(a, b) for a, b in PARTNER if a % 2 == 1]
 ACROSS = over_all(across_y)
 SWAP = over_all(lambda y, x, z, hi, core: (y, x, z, hi, 1 - core))
 
@@ -505,14 +505,14 @@
     late, early_sums = lax.optimization_barrier((late, early_sums))
     late_sums = experts(late, own)
     near, late_sums = lax.optimization_barrier((near, late_sums))
-    far_a, far_b, op_b, on_a = experts(late, near, late_sums)
-    far_a, far_b, op_b, on_a, early, early_sums = lax.optimization_barrier(
-        (far_a, far_b, op_b, on_a, early, early_sums)
-    )
+    far_a, far_b = experts(late[:2], near, late_sums[:2])
+    far_a, far_b, early, early_sums = lax.optimization_barrier((far_a, far_b, early, early_sums))
     far_a, far_b = permute(far_a, NEXT), permute(far_b, BACK)
-    oo_a, oo_b, op_a, on_b = experts(early, near, early_sums)
-    far_a, far_b, oo_a, oo_b, op_a, on_b = lax.optimization_barrier(
-        (far_a, far_b, oo_a, oo_b, op_a, on_b)
+    oo_a, oo_b, op_a, on_b, op_b, on_a = experts(
+        early + late[2:], near, early_sums + late_sums[2:]
+    )
+    far_a, far_b, oo_a, oo_b, op_a, on_b, op_b, on_a = lax.optimization_barrier(
+        (far_a, far_b, oo_a, oo_b, op_a, on_b, op_b, on_a)
     )
     from_prev = permute(jnp.stack([add(on_a, far_a), on_b]), NEXT)
     from_next = permute(jnp.stack([op_a, add(op_b, far_b)]), BACK)

time: 203 us -> 203 us (level)
  transfers between devices with their start and end apart: 21 -> 21, of which waited for: 14 -> 13; matrix products, arithmetic and copies ran while one was open for 0% -> 0% of each run, Pallas kernels for 15% -> 16%
where the time goes in v2:
time: 203 us; the launch traced here: 202 us
  blocking collectives  63.2 us (31%)
  waiting for transfers between devices  60.6 us (30%)
  Pallas kernels  37.2 us (18%)
  starting transfers between devices  36.7 us (18%)
  local copies, waits for them, and re-layouts  3.37 us (2%)
    ppermute x16, waiting for transfers between devices, permute(): return lax.ppermute(v, ('ctx', 'exp'), pairs)  44.6 us
    ppermute x16, starting transfers between devices, permute(): return lax.ppermute(v, ('ctx', 'exp'), pairs)  29.2 us
    all_to_all x1, blocking collectives, on_device(): lax.all_to_all(summed, 'exp', split_axis=0, concat_axis=0, tiled=True)  22.4 us
    all_to_all x1, blocking collectives, on_device(): lax.all_to_all(packed, 'ctx', split_axis=0, concat_axis=0, tiled=True, ax...  20.5 us
    all_to_all x1, blocking collectives, on_device(): lax.all_to_all(send, 'exp', split_axis=0, concat_axis=0, tiled=True)  20.2 us
    pallas_call x4, Pallas kernels, experts(): pl.pallas_call(functools.partial(expert_kernel, sizes, near), out_shape=t...  16.4 us
    ppermute x2, waiting for transfers between devices, go_right(): return lax.ppermute(v, 'ctx', RIGHT)  14.2 us
    pallas_call x3, Pallas kernels, attend(): pl.pallas_call(functools.partial(attend_kernel, steps), out_shape=jax.Sha...  12.5 us
  transfers between devices with their start and end apart: 21, of which 13 were waited for; matrix products, arithmetic and copies ran while one was open for 0% of the time, Pallas kernels for 16%

profile of v2, /device:TPU:1, one launch (start us, length us, event | category | flops | bytes accessed | tf_op | source)
XLA Modules:
  0.0 202.2 jit_solution(5269564600712212151)
XLA Ops:
  0.0 1.6 dynamic-slice_bitcast_fusion
  1.7 0.4 copy-done.3
  2.0 0.8 collective-permute-start
  2.8 3.6 %collective-permute-start.2 = (bf16[1440,512]{1,0:T(8,128)(2,1)S(1)}, bf16[1440,512]{1,0:T(8,128)(2,1)S(1)}, u32[]{:S(2)}, u32[]{:S(2)}) collective-permute-start(bf16[1440,512]{1,0:T(8,128)(2,1)S(1)} %dynamic-slice_bitcast_fusion), channel_id=1, source_target_pairs={{0,66},{1,67},{2,64},{3,65},{4,70},{5,71},{6,68},{7,69},{8,74},{9,... | collective-permute-start | bytes 4423688 | tf_op jit(solution)/shard_map/ppermute | solution.py:484
  6.5 1.2 copy-done.4
  7.7 0.2 shard_map.127
  7.9 0.0 copy-start.1
  8.0 20.5 %all_to_all.28.pack_ref = bf16[4,144,1280]{2,1,0:T(8,128)(2,1)S(1)} all-to-all(bf16[4,144,1280]{2,1,0:T(8,128)(2,1)S(1)} %shard_map.127), channel_id=1, replica_groups={{0,16,32,48},{64,80,96,112},{1,17,33,49},{65,81,97,113},{2,18,34,50},{6..., dimensions={0} | all-to-all | bytes 2949120 | tf_op jit(solution)/shard_map/all_to_all | solution.py:548
  28.5 1.3 collective-permute-start.1
  29.8 2.3 %collective-permute-start.4 = (bf16[360,2880]{1,0:T(8,128)(2,1)S(1)}, bf16[360,2880]{1,0:T(8,128)(2,1)S(1)}, u32[]{:S(2)}, u32[]{:S(2)}) collective-permute-start(bf16[360,2880]{1,0:T(8,128)(2,1)S(1)} %bitcast.56), channel_id=1, source_target_pairs={{1,17},{3,19},{5,21},{7,23},{9,25},{11,27},{13,29},{15,31},{17,1},... | collective-permute-start | bytes 6220808 | tf_op jit(solution)/shard_map/ppermute | solution.py:484
  32.2 0.0 copy-start.11
  32.2 0.3 shard_map.128
  32.5 0.0 copy-start
  32.5 3.0 %collective-permute-done.2.w_first = bf16[1440,512]{1,0:T(8,128)(2,1)S(1)} collective-permute-done((bf16[1440,512]{1,0:T(8,128)(2,1)S(1)}, bf16[1440,512]{1,0:T(8,128)(2,1)S(1)}, u32[]{:S(2)}, u32[]{:S(2)}) %collective-permute-start.2) | collective-permute-done | bytes 1474592 | tf_op jit(solution)/shard_map/ppermute | solution.py:484
  35.5 4.2 %collective-permute-start.3 = (bf16[1440,512]{1,0:T(8,128)(2,1)S(1)}, bf16[1440,512]{1,0:T(8,128)(2,1)S(1)}, u32[]{:S(2)}, u32[]{:S(2)}) collective-permute-start(bf16[1440,512]{1,0:T(8,128)(2,1)S(1)} %collective-permute-done.2.w_first), channel_id=1, source_target_pairs={{0,1},{1,0},{2,3},{3,2},{4,5},{5,4},{6,7},{7,6},{8,9},{9,8},{10,11... | collective-permute-start | bytes 4423688 | tf_op jit(solution)/shard_map/ppermute | solution.py:484
  39.7 0.9 collective-permute-start.9
  40.7 3.5 %shard_map.129.attn = bf16[128,1024]{1,0:T(8,128)(2,1)S(1)} custom-call(f32[64]{0:T(128)S(1)} %copy-done.11, bf16[4,144,1280]{2,1,0:T(8,128)(2,1)S(1)} %all_to_all.28.pack_ref, bf16[4,144,256]{2,1,0:T(8,128)(2,1)S(1)} %collective-permute-done.1.low_ref), custom_call_target="tpu_custom_call" | custom-call | flops 2147483648 | bytes 4194304 | tf_op jit(solution)/shard_map/pallas_call | solution.py:209
  44.2 1.7 shard_map.130
  45.9 1.8 collective-permute-start.5
  47.7 1.7 collective-permute-start.6
  49.4 6.0 %shard_map.131.attn = bf16[256,1024]{1,0:T(8,128)(2,1)S(1)} custom-call(f32[64]{0:T(128)S(1)} %copy-done.11, bf16[4,144,1280]{2,1,0:T(8,128)(2,1)S(1)} %all_to_all.28.pack_ref, bf16[4,144,256]{2,1,0:T(8,128)(2,1)S(1)} %collective-permute-done.1.low_ref), custom_call_target="tpu_custom_call" | custom-call | flops 2147483648 | bytes 4194304 | tf_op jit(solution)/shard_map/pallas_call | solution.py:209
  55.4 4.1 %collective-permute-done.4.refs_3_.refs_7_ = bf16[360,2880]{1,0:T(8,128)(2,1)S(1)} collective-permute-done((bf16[360,2880]{1,0:T(8,128)(2,1)S(1)}, bf16[360,2880]{1,0:T(8,128)(2,1)S(1)}, u32[]{:S(2)}, u32[]{:S(2)}) %collective-permute-start.4) | collective-permute-done | bytes 2073632 | tf_op jit(solution)/shard_map/ppermute | solution.py:484
  59.5 3.8 %collective-permute-done.5.refs_0_ = bf16[1440,128]{1,0:T(8,128)(2,1)S(1)} collective-permute-done((bf16[1440,128]{1,0:T(8,128)(2,1)S(1)}, bf16[1440,128]{1,0:T(8,128)(2,1)S(1)}, u32[]{:S(2)}, u32[]{:S(2)}) %collective-permute-start.5) | collective-permute-done | bytes 368672 | tf_op jit(solution)/shard_map/ppermute | solution.py:41
  63.3 1.8 collective-permute-done.6.refs_1_
  65.0 1.7 shard_map.132
  66.8 0.5 collective-permute-start.7
  67.3 2.3 %collective-permute-start.8 = (bf16[2880,128]{1,0:T(8,128)(2,1)S(1)}, bf16[2880,128]{1,0:T(8,128)(2,1)S(1)}, u32[]{:S(2)}, u32[]{:S(2)}) collective-permute-start(bf16[2880,128]{1,0:T(8,128)(2,1)S(1)} %get-tuple-element.104), channel_id=1, source_target_pairs={{0,48},{16,0},{32,16},{48,32},{64,112},{80,64},{96,80},{112,96},{1... | collective-permute-start | bytes 2211848 | tf_op jit(solution)/shard_map/ppermute | solution.py:45
  69.5 3.0 %shard_map.133.attn = bf16[128,1024]{1,0:T(8,128)(2,1)S(1)} custom-call(f32[64]{0:T(128)S(1)} %copy-done.11, bf16[4,144,1280]{2,1,0:T(8,128)(2,1)S(1)} %all_to_all.28.pack_ref, bf16[4,144,256]{2,1,0:T(8,128)(2,1)S(1)} %collective-permute-done.1.low_ref), custom_call_target="tpu_custom_call" | custom-call | flops 2147483648 | bytes 4194304 | tf_op jit(solution)/shard_map/pallas_call | solution.py:209
  72.6 0.0 copy-start.12
  72.6 1.7 shard_map.134
  74.3 10.5 %collective-permute-done.7.left = bf16[2880,128]{1,0:T(8,128)(2,1)S(1)} collective-permute-done((bf16[2880,128]{1,0:T(8,128)(2,1)S(1)}, bf16[2880,128]{1,0:T(8,128)(2,1)S(1)}, u32[]{:S(2)}, u32[]{:S(2)}) %collective-permute-start.7) | collective-permute-done | bytes 737312 | tf_op jit(solution)/shard_map/ppermute | solution.py:41
  84.8 2.5 %collective-permute-start.16 = (bf16[728,2880]{1,0:T(8,128)(2,1)S(1)}, bf16[728,2880]{1,0:T(8,128)(2,1)S(1)}, u32[]{:S(2)}, u32[]{:S(2)}) collective-permute-start(bf16[728,2880]{1,0:T(8,128)(2,1)S(1)} %shard_map.128), channel_id=1, source_target_pairs={{1,17},{3,19},{5,21},{7,23},{9,25},{11,27},{13,29},{15,31},{17,1},... | collective-permute-start | bytes 12579848 | tf_op jit(solution)/shard_map/ppermute | solution.py:484
  87.3 1.2 shard_map.135
  88.4 20.2 %all_to_all.29 = bf16[16,8,2880]{2,1,0:T(8,128)(2,1)S(1)} all-to-all(bf16[16,8,2880]{2,1,0:T(8,128)(2,1)S(1)} %bitcast.60), channel_id=1, replica_groups=mesh['ctx'=8,'exp'=16] {'exp'}, dimensions={0} | all-to-all | bytes 1474560 | tf_op jit(solution)/shard_map/all_to_all | solution.py:581
  108.7 0.1 fusion.4
  108.7 0.1 collective-permute-start.12
  108.8 2.7 %collective-permute-start.10 = (bf16[64,2880]{1,0:T(8,128)(2,1)S(1)}, bf16[64,2880]{1,0:T(8,128)(2,1)S(1)}, u32[]{:S(2)}, u32[]{:S(2)}) collective-permute-start(bf16[64,2880]{1,0:T(8,128)(2,1)S(1)} %get-tuple-element.147.refs_0_), channel_id=1, source_target_pairs={{0,16},{1,49},{2,18},{3,51},{4,20},{5,53},{6,22},{7,55},{8,24},{9,... | collective-permute-start | bytes 1105928 | tf_op jit(solution)/shard_map/ppermute | solution.py:484
  111.6 1.4 collective-permute-start.14
  112.9 0.1 collective-permute-start.15
  113.0 3.4 %collective-permute-done.12.refs_3_ = bf16[64,2880]{1,0:T(8,128)(2,1)S(1)} collective-permute-done((bf16[64,2880]{1,0:T(8,128)(2,1)S(1)}, bf16[64,2880]{1,0:T(8,128)(2,1)S(1)}, u32[]{:S(2)}, u32[]{:S(2)}) %collective-permute-start.12) | collective-permute-done | bytes 368672 | tf_op jit(solution)/shard_map/ppermute | solution.py:484
  116.5 1.3 collective-permute-start.13
  117.8 1.1 collective-permute-done.10.refs_2_
  118.9 3.4 %collective-permute-start.11 = (bf16[64,2880]{1,0:T(8,128)(2,1)S(1)}, bf16[64,2880]{1,0:T(8,128)(2,1)S(1)}, u32[]{:S(2)}, u32[]{:S(2)}) collective-permute-start(bf16[64,2880]{1,0:T(8,128)(2,1)S(1)} %collective-permute-done.10.refs_2_), channel_id=1, source_target_pairs={{0,16},{1,49},{2,18},{3,51},{4,20},{5,53},{6,22},{7,55},{8,24},{9,... | collective-permute-start | bytes 1105928 | tf_op jit(solution)/shard_map/ppermute | solution.py:484
  122.3 3.4 %shard_map.136 = (bf16[64,2880]{1,0:T(8,128)(2,1)S(1)}, bf16[64,2880]{1,0:T(8,128)(2,1)S(1)}, bf16[64,2880]{1,0:T(8,128)(2,1)S(1)}, bf16[64,2880]{1,0:T(8,128)(2,1)S(1)}) custom-call(bf16[64,2880]{1,0:T(8,128)(2,1)S(1)} %get-tuple-element.147.refs_0_, bf16[64,2880]{1,0:T(8,128)(2,1)S(1)} %get-tuple-element.148.refs_1_, ...), custom_call_target="tpu_custom_call" | custom-call | flops 1592524800 | bytes 4194304 | tf_op jit(solution)/shard_map/pallas_call | solution.py:441
  125.7 1.3 collective-permute-done.14.refs_2_.refs_4_
  127.0 5.9 %collective-permute-done.13.refs_1_ = bf16[64,2880]{1,0:T(8,128)(2,1)S(1)} collective-permute-done((bf16[64,2880]{1,0:T(8,128)(2,1)S(1)}, bf16[64,2880]{1,0:T(8,128)(2,1)S(1)}, u32[]{:S(2)}, u32[]{:S(2)}) %collective-permute-start.13) | collective-permute-done | bytes 368672 | tf_op jit(solution)/shard_map/ppermute | solution.py:484
  132.9 2.1 %collective-permute-done.11.refs_0_ = bf16[64,2880]{1,0:T(8,128)(2,1)S(1)} collective-permute-done((bf16[64,2880]{1,0:T(8,128)(2,1)S(1)}, bf16[64,2880]{1,0:T(8,128)(2,1)S(1)}, u32[]{:S(2)}, u32[]{:S(2)}) %collective-permute-start.11) | collective-permute-done | bytes 368672 | tf_op jit(solution)/shard_map/ppermute | solution.py:484
  135.0 3.4 %shard_map.137 = (bf16[64,2880]{1,0:T(8,128)(2,1)S(1)}, bf16[64,2880]{1,0:T(8,128)(2,1)S(1)}, bf16[64,2880]{1,0:T(8,128)(2,1)S(1)}, bf16[64,2880]{1,0:T(8,128)(2,1)S(1)}) custom-call(bf16[64,2880]{1,0:T(8,128)(2,1)S(1)} %collective-permute-done.11.refs_0_, bf16[64,2880]{1,0:T(8,128)(2,1)S(1)} %collective-permute-done.13.refs_1_, ...), custom_call_target="tpu_custom_call" | custom-call | flops 1592524800 | bytes 4194304 | tf_op jit(solution)/shard_map/pallas_call | solution.py:441
  138.4 8.7 %collective-permute-done.16.refs_5_.refs_9_ = bf16[728,2880]{1,0:T(8,128)(2,1)S(1)} collective-permute-done((bf16[728,2880]{1,0:T(8,128)(2,1)S(1)}, bf16[728,2880]{1,0:T(8,128)(2,1)S(1)}, u32[]{:S(2)}, u32[]{:S(2)}) %collective-permute-start.16) | collective-permute-done | bytes 4193312 | tf_op jit(solution)/shard_map/ppermute | solution.py:484
  147.1 3.4 %shard_map.138 = (bf16[64,2880]{1,0:T(8,128)(2,1)S(1)}, bf16[64,2880]{1,0:T(8,128)(2,1)S(1)}) custom-call(bf16[64,2880]{1,0:T(8,128)(2,1)S(1)} %collective-permute-done.11.refs_0_, bf16[64,2880]{1,0:T(8,128)(2,1)S(1)} %collective-permute-done.13.refs_1_, bf16[360,2880]{1,0:T(8,128)(2,1)S(1)} %collective-permute-done.refs_2_.refs_6_, ...), custom_call_target="tpu_custom_call" | custom-call | flops 796262400 | bytes 4194304 | tf_op jit(solution)/shard_map/pallas_call | solution.py:441
  150.6 3.0 %collective-permute-start.17 = (bf16[64,2880]{1,0:T(8,128)(2,1)S(1)}, bf16[64,2880]{1,0:T(8,128)(2,1)S(1)}, u32[]{:S(2)}, u32[]{:S(2)}) collective-permute-start(bf16[64,2880]{1,0:T(8,128)(2,1)S(1)} %get-tuple-element.145), channel_id=1, source_target_pairs={{0,16},{1,49},{2,18},{3,51},{4,20},{5,53},{6,22},{7,55},{8,24},{9,... | collective-permute-start | bytes 1105928 | tf_op jit(solution)/shard_map/ppermute | solution.py:484
  153.6 6.1 %shard_map.139 = (bf16[64,2880]{1,0:T(8,128)(2,1)S(1)}, bf16[64,2880]{1,0:T(8,128)(2,1)S(1)}, bf16[64,2880]{1,0:T(8,128)(2,1)S(1)}, bf16[64,2880]{1,0:T(8,128)(2...) custom-call(bf16[64,2880]{1,0:T(8,128)(2,1)S(1)} %get-tuple-element.147.refs_0_, ...), custom_call_target="tpu_custom_call" | custom-call | flops 2388787200 | bytes 4194304 | tf_op jit(solution)/shard_map/pallas_call | solution.py:441
  159.7 1.5 collective-permute-done.18
  161.2 0.1 fusion.3
  161.3 0.1 pad_maximum_fusion.1
  161.4 0.1 collective-permute-start.20
  161.5 0.1 fusion.2
  161.6 0.1 pad_maximum_fusion
  161.7 2.7 %collective-permute-start.19 = (bf16[2,64,2880]{2,1,0:T(8,128)(2,1)S(1)}, bf16[2,64,2880]{2,1,0:T(8,128)(2,1)S(1)}, u32[]{:S(2)}, u32[]{:S(2)}) collective-permute-start(bf16[2,64,2880]{2,1,0:T(8,128)(2,1)S(1)} %pad_maximum_fusion), channel_id=1, source_target_pairs={{0,16},{1,49},{2,18},{3,51},{4,20},{5,53},{6,22},{7,55},{8,24},{9,... | collective-permute-start | bytes 2211848 | tf_op jit(solution)/shard_map/ppermute | solution.py:484
  164.4 13.4 %collective-permute-done.20 = bf16[2,64,2880]{2,1,0:T(8,128)(2,1)S(1)} collective-permute-done((bf16[2,64,2880]{2,1,0:T(8,128)(2,1)S(1)}, bf16[2,64,2880]{2,1,0:T(8,128)(2,1)S(1)}, u32[]{:S(2)}, u32[]{:S(2)}) %collective-permute-start.20) | collective-permute-done | bytes 737312 | tf_op jit(solution)/shard_map/ppermute | solution.py:484
  177.8 0.3 fusion.1
  178.1 0.1 maximum_bitcast_fusion
  178.2 22.4 %all_to_all.30 = bf16[16,8,2880]{2,1,0:T(8,128)(2,1)S(1)} all-to-all(bf16[16,8,2880]{2,1,0:T(8,128)(2,1)S(1)} %maximum_bitcast_fusion), channel_id=1, replica_groups=mesh['ctx'=8,'exp'=16] {'exp'}, dimensions={0} | all-to-all | bytes 1474560 | tf_op jit(solution)/shard_map/all_to_all | solution.py:584
  200.6 1.6 shard_map.140
  (31 shorter events, 0.1 us)
Async XLA Ops:
  0.0 2.0 %copy-start.3 = (bf16[1,2880,360]{1,2,0:T(8,128)(2,1)S(1)}, bf16[1,2880,360]{1,2,0:T(8,128)(2,1)}, u32[]{:S(2)}) copy-start(bf16[1,2880,360]{1,2,0:T(8,128)(2,1)} %param.21) | copy-start | bytes 6220804
  0.0 6.5 %copy-start.10 = (s32[128]{0:T(128)S(1)}, s32[128]{0:T(128)}, u32[]{:S(2)}) copy-start(s32[128]{0:T(128)} %param.18) | copy-start | bytes 1540
  0.0 6.5 %copy-start.7 = (bf16[128,512]{1,0:T(8,128)(2,1)S(1)}, bf16[128,512]{1,0:T(8,128)(2,1)}, u32[]{:S(2)}) copy-start(bf16[128,512]{1,0:T(8,128)(2,1)} %v_ref.1) | copy-start | bytes 393220
  0.0 6.5 %copy-start.6 = (bf16[128,512]{1,0:T(8,128)(2,1)S(1)}, bf16[128,512]{1,0:T(8,128)(2,1)}, u32[]{:S(2)}) copy-start(bf16[128,512]{1,0:T(8,128)(2,1)} %k_ref.1) | copy-start | bytes 393220
  2.0 26.5 %collective-permute-start = (bf16[360,2880]{1,0:T(8,128)(2,1)S(1)}, bf16[360,2880]{1,0:T(8,128)(2,1)S(1)}, u32[]{:S(2)}, u32[]{:S(2)}) collective-permute-start(bf16[360,2880]{1,0:T(8,128)(2,1)S(1)} %bitcast.55), channel_id=1, source_target_pairs={{0,64},{2,66},{4,68},{6,70},{8,72},{10,74},{12,76},{14,78},{16,80}... | collective-permute-start | bytes 6220808 | tf_op jit(solution)/shard_map/ppermute | solution.py:484
  2.8 32.7 %collective-permute-start.2 = (bf16[1440,512]{1,0:T(8,128)(2,1)S(1)}, bf16[1440,512]{1,0:T(8,128)(2,1)S(1)}, u32[]{:S(2)}, u32[]{:S(2)}) collective-permute-start(bf16[1440,512]{1,0:T(8,128)(2,1)S(1)} %dynamic-slice_bitcast_fusion), channel_id=1, source_target_pairs={{0,66},{1,67},{2,64},{3,65},{4,70},{5,71},{6,68},{7,69},{8,74},{9,... | collective-permute-start | bytes 4423688 | tf_op jit(solution)/shard_map/ppermute | solution.py:484
  6.5 1.2 copy-start.4
  7.7 24.5 %copy-start.2 = (bf16[1,360,2880]{2,1,0:T(8,128)(2,1)S(1)}, bf16[1,360,2880]{2,1,0:T(8,128)(2,1)}, u32[]{:S(2)}) copy-start(bf16[1,360,2880]{2,1,0:T(8,128)(2,1)} %param.23) | copy-start | bytes 6220804
  7.9 24.2 %copy-start.1 = (bf16[1,2880,360]{1,2,0:T(8,128)(2,1)S(1)}, bf16[1,2880,360]{1,2,0:T(8,128)(2,1)}, u32[]{:S(2)}) copy-start(bf16[1,2880,360]{1,2,0:T(8,128)(2,1)} %param.22) | copy-start | bytes 6220804
  28.5 7.0 %collective-permute-start.1 = (bf16[4,144,256]{2,1,0:T(8,128)(2,1)S(1)}, bf16[4,144,256]{2,1,0:T(8,128)(2,1)S(1)}, u32[]{:S(2)}, u32[]{:S(2)}) collective-permute-start(bf16[4,144,256]{2,1,0:T(8,128)(2,1)S(1)} %slice.21), channel_id=1, source_target_pairs={{0,64},{16,80},{32,96},{48,112},{1,65},{17,81},{33,97},{49,113},{2... | collective-permute-start | bytes 884744 | tf_op jit(solution)/shard_map/ppermute | solution.py:557
  29.8 29.7 %collective-permute-start.4 = (bf16[360,2880]{1,0:T(8,128)(2,1)S(1)}, bf16[360,2880]{1,0:T(8,128)(2,1)S(1)}, u32[]{:S(2)}, u32[]{:S(2)}) collective-permute-start(bf16[360,2880]{1,0:T(8,128)(2,1)S(1)} %bitcast.56), channel_id=1, source_target_pairs={{1,17},{3,19},{5,21},{7,23},{9,25},{11,27},{13,29},{15,31},{17,1},... | collective-permute-start | bytes 6220808 | tf_op jit(solution)/shard_map/ppermute | solution.py:484
  32.2 8.5 %copy-start.11 = (f32[64]{0:T(128)S(1)}, f32[64]{0:T(128)}, u32[]{:S(2)}) copy-start(f32[64]{0:T(128)} %sinks.5) | copy-start | bytes 772
  32.5 11.7 %copy-start = (bf16[512,2880]{0,1:T(8,128)(2,1)S(1)}, bf16[512,2880]{0,1:T(8,128)(2,1)}, u32[]{:S(2)}) copy-start(bf16[512,2880]{0,1:T(8,128)(2,1)} %param.20) | copy-start | bytes 8847364
  35.5 8.6 %collective-permute-start.3 = (bf16[1440,512]{1,0:T(8,128)(2,1)S(1)}, bf16[1440,512]{1,0:T(8,128)(2,1)S(1)}, u32[]{:S(2)}, u32[]{:S(2)}) collective-permute-start(bf16[1440,512]{1,0:T(8,128)(2,1)S(1)} %collective-permute-done.2.w_first), channel_id=1, source_target_pairs={{0,1},{1,0},{2,3},{3,2},{4,5},{5,4},{6,7},{7,6},{8,9},{9,8},{10,11... | collective-permute-start | bytes 4423688 | tf_op jit(solution)/shard_map/ppermute | solution.py:484
  39.7 69.0 %collective-permute-start.9 = (bf16[728,2880]{1,0:T(8,128)(2,1)S(1)}, bf16[728,2880]{1,0:T(8,128)(2,1)S(1)}, u32[]{:S(2)}, u32[]{:S(2)}) collective-permute-start(bf16[728,2880]{1,0:T(8,128)(2,1)S(1)} %shard_map.128), channel_id=1, source_target_pairs={{0,64},{2,66},{4,68},{6,70},{8,72},{10,74},{12,76},{14,78},{16,80}... | collective-permute-start | bytes 12579848 | tf_op jit(solution)/shard_map/ppermute | solution.py:484
  45.9 17.4 %collective-permute-start.5 = (bf16[1440,128]{1,0:T(8,128)(2,1)S(1)}, bf16[1440,128]{1,0:T(8,128)(2,1)S(1)}, u32[]{:S(2)}, u32[]{:S(2)}) collective-permute-start(bf16[1440,128]{1,0:T(8,128)(2,1)S(1)} %get-tuple-element.99), channel_id=1, source_target_pairs={{0,16},{16,32},{32,48},{48,0},{64,80},{80,96},{96,112},{112,64},{1... | collective-permute-start | bytes 1105928 | tf_op jit(solution)/shard_map/ppermute | solution.py:41
  47.7 17.4 %collective-permute-start.6 = (bf16[1440,128]{1,0:T(8,128)(2,1)S(1)}, bf16[1440,128]{1,0:T(8,128)(2,1)S(1)}, u32[]{:S(2)}, u32[]{:S(2)}) collective-permute-start(bf16[1440,128]{1,0:T(8,128)(2,1)S(1)} %get-tuple-element.100), channel_id=1, source_target_pairs={{0,48},{16,0},{32,16},{48,32},{64,112},{80,64},{96,80},{112,96},{1... | collective-permute-start | bytes 1105928 | tf_op jit(solution)/shard_map/ppermute | solution.py:45
  66.8 18.0 %collective-permute-start.7 = (bf16[2880,128]{1,0:T(8,128)(2,1)S(1)}, bf16[2880,128]{1,0:T(8,128)(2,1)S(1)}, u32[]{:S(2)}, u32[]{:S(2)}) collective-permute-start(bf16[2880,128]{1,0:T(8,128)(2,1)S(1)} %get-tuple-element.103), channel_id=1, source_target_pairs={{0,16},{16,32},{32,48},{48,0},{64,80},{80,96},{96,112},{112,64},{1... | collective-permute-start | bytes 2211848 | tf_op jit(solution)/shard_map/ppermute | solution.py:41
  67.3 17.5 %collective-permute-start.8 = (bf16[2880,128]{1,0:T(8,128)(2,1)S(1)}, bf16[2880,128]{1,0:T(8,128)(2,1)S(1)}, u32[]{:S(2)}, u32[]{:S(2)}) collective-permute-start(bf16[2880,128]{1,0:T(8,128)(2,1)S(1)} %get-tuple-element.104), channel_id=1, source_target_pairs={{0,48},{16,0},{32,16},{48,32},{64,112},{80,64},{96,80},{112,96},{1... | collective-permute-start | bytes 2211848 | tf_op jit(solution)/shard_map/ppermute | solution.py:45
  72.6 14.6 %copy-start.12 = (f32[2880]{0:T(1024)S(1)}, f32[2880]{0:T(1024)}, u32[]{:S(2)}) copy-start(f32[2880]{0:T(1024)} %param.19) | copy-start | bytes 34564
  72.6 14.7 %copy-start.5 = (bf16[128,2880]{0,1:T(8,128)(2,1)S(1)}, bf16[128,2880]{0,1:T(8,128)(2,1)}, u32[]{:S(2)}) copy-start(bf16[128,2880]{0,1:T(8,128)(2,1)} %param.13) | copy-start | bytes 2211844
  72.6 14.7 %copy-start.8 = (s32[128,4]{0,1:T(4,128)S(1)}, s32[128,4]{0,1:T(4,128)}, u32[]{:S(2)}) copy-start(s32[128,4]{0,1:T(4,128)} %param.24) | copy-start | bytes 6148
  84.8 62.3 %collective-permute-start.16 = (bf16[728,2880]{1,0:T(8,128)(2,1)S(1)}, bf16[728,2880]{1,0:T(8,128)(2,1)S(1)}, u32[]{:S(2)}, u32[]{:S(2)}) collective-permute-start(bf16[728,2880]{1,0:T(8,128)(2,1)S(1)} %shard_map.128), channel_id=1, source_target_pairs={{1,17},{3,19},{5,21},{7,23},{9,25},{11,27},{13,29},{15,31},{17,1},... | collective-permute-start | bytes 12579848 | tf_op jit(solution)/shard_map/ppermute | solution.py:484
  108.7 7.7 %collective-permute-start.12 = (bf16[64,2880]{1,0:T(8,128)(2,1)S(1)}, bf16[64,2880]{1,0:T(8,128)(2,1)S(1)}, u32[]{:S(2)}, u32[]{:S(2)}) collective-permute-start(bf16[64,2880]{1,0:T(8,128)(2,1)S(1)} %get-tuple-element.148.refs_1_), channel_id=1, source_target_pairs={{16,0},{49,1},{18,2},{51,3},{20,4},{53,5},{22,6},{55,7},{24,8},{57... | collective-permute-start | bytes 1105928 | tf_op jit(solution)/shard_map/ppermute | solution.py:484
  108.8 10.1 %collective-permute-start.10 = (bf16[64,2880]{1,0:T(8,128)(2,1)S(1)}, bf16[64,2880]{1,0:T(8,128)(2,1)S(1)}, u32[]{:S(2)}, u32[]{:S(2)}) collective-permute-start(bf16[64,2880]{1,0:T(8,128)(2,1)S(1)} %get-tuple-element.147.refs_0_), channel_id=1, source_target_pairs={{0,16},{1,49},{2,18},{3,51},{4,20},{5,53},{6,22},{7,55},{8,24},{9,... | collective-permute-start | bytes 1105928 | tf_op jit(solution)/shard_map/ppermute | solution.py:484
  111.6 15.4 %collective-permute-start.14 = (bf16[64,2880]{1,0:T(8,128)(2,1)S(1)}, bf16[64,2880]{1,0:T(8,128)(2,1)S(1)}, u32[]{:S(2)}, u32[]{:S(2)}) collective-permute-start(bf16[64,2880]{1,0:T(8,128)(2,1)S(1)} %get-tuple-element.148.refs_1_), channel_id=1, source_target_pairs={{0,16},{1,49},{2,18},{3,51},{4,20},{5,53},{6,22},{7,55},{8,24},{9,... | collective-permute-start | bytes 1105928 | tf_op jit(solution)/shard_map/ppermute | solution.py:484
  112.9 14.0 %collective-permute-start.15 = (bf16[64,2880]{1,0:T(8,128)(2,1)S(1)}, bf16[64,2880]{1,0:T(8,128)(2,1)S(1)}, u32[]{:S(2)}, u32[]{:S(2)}) collective-permute-start(bf16[64,2880]{1,0:T(8,128)(2,1)S(1)} %get-tuple-element.147.refs_0_), channel_id=1, source_target_pairs={{16,0},{49,1},{18,2},{51,3},{20,4},{53,5},{22,6},{55,7},{24,8},{57... | collective-permute-start | bytes 1105928 | tf_op jit(solution)/shard_map/ppermute | solution.py:484
  116.5 16.4 %collective-permute-start.13 = (bf16[64,2880]{1,0:T(8,128)(2,1)S(1)}, bf16[64,2880]{1,0:T(8,128)(2,1)S(1)}, u32[]{:S(2)}, u32[]{:S(2)}) collective-permute-start(bf16[64,2880]{1,0:T(8,128)(2,1)S(1)} %collective-permute-done.12.refs_3_), channel_id=1, source_target_pairs={{16,0},{49,1},{18,2},{51,3},{20,4},{53,5},{22,6},{55,7},{24,8},{57... | collective-permute-start | bytes 1105928 | tf_op jit(solution)/shard_map/ppermute | solution.py:484
  118.9 16.1 %collective-permute-start.11 = (bf16[64,2880]{1,0:T(8,128)(2,1)S(1)}, bf16[64,2880]{1,0:T(8,128)(2,1)S(1)}, u32[]{:S(2)}, u32[]{:S(2)}) collective-permute-start(bf16[64,2880]{1,0:T(8,128)(2,1)S(1)} %collective-permute-done.10.refs_2_), channel_id=1, source_target_pairs={{0,16},{1,49},{2,18},{3,51},{4,20},{5,53},{6,22},{7,55},{8,24},{9,... | collective-permute-start | bytes 1105928 | tf_op jit(solution)/shard_map/ppermute | solution.py:484
  150.6 9.2 %collective-permute-start.17 = (bf16[64,2880]{1,0:T(8,128)(2,1)S(1)}, bf16[64,2880]{1,0:T(8,128)(2,1)S(1)}, u32[]{:S(2)}, u32[]{:S(2)}) collective-permute-start(bf16[64,2880]{1,0:T(8,128)(2,1)S(1)} %get-tuple-element.145), channel_id=1, source_target_pairs={{0,16},{1,49},{2,18},{3,51},{4,20},{5,53},{6,22},{7,55},{8,24},{9,... | collective-permute-start | bytes 1105928 | tf_op jit(solution)/shard_map/ppermute | solution.py:484
  153.6 7.7 %collective-permute-start.18 = (bf16[64,2880]{1,0:T(8,128)(2,1)S(1)}, bf16[64,2880]{1,0:T(8,128)(2,1)S(1)}, u32[]{:S(2)}, u32[]{:S(2)}) collective-permute-start(bf16[64,2880]{1,0:T(8,128)(2,1)S(1)} %get-tuple-element.146), channel_id=1, source_target_pairs={{16,0},{49,1},{18,2},{51,3},{20,4},{53,5},{22,6},{55,7},{24,8},{57... | collective-permute-start | bytes 1105928 | tf_op jit(solution)/shard_map/ppermute | solution.py:484
  161.4 16.4 %collective-permute-start.20 = (bf16[2,64,2880]{2,1,0:T(8,128)(2,1)S(1)}, bf16[2,64,2880]{2,1,0:T(8,128)(2,1)S(1)}, u32[]{:S(2)}, u32[]{:S(2)}) collective-permute-start(bf16[2,64,2880]{2,1,0:T(8,128)(2,1)S(1)} %pad_maximum_fusion.1), channel_id=1, source_target_pairs={{16,0},{49,1},{18,2},{51,3},{20,4},{53,5},{22,6},{55,7},{24,8},{57... | collective-permute-start | bytes 2211848 | tf_op jit(solution)/shard_map/ppermute | solution.py:484
  161.7 16.1 %collective-permute-start.19 = (bf16[2,64,2880]{2,1,0:T(8,128)(2,1)S(1)}, bf16[2,64,2880]{2,1,0:T(8,128)(2,1)S(1)}, u32[]{:S(2)}, u32[]{:S(2)}) collective-permute-start(bf16[2,64,2880]{2,1,0:T(8,128)(2,1)S(1)} %pad_maximum_fusion), channel_id=1, source_target_pairs={{0,16},{1,49},{2,18},{3,51},{4,20},{5,53},{6,22},{7,55},{8,24},{9,... | collective-permute-start | bytes 2211848 | tf_op jit(solution)/shard_map/ppermute | solution.py:484
  178.1 22.5 %copy-start.9 = (f32[128,4]{0,1:T(4,128)S(1)}, f32[128,4]{0,1:T(4,128)}, u32[]{:S(2)}) copy-start(f32[128,4]{0,1:T(4,128)} %param.25) | copy-start | bytes 6148

commit v3 on v2

--- a/solution.py
+++ b/solution.py
@@ -19,7 +19,7 @@
 NX = 4
 QUARTER = ALL_EXPERTS // TOPK
 WINDOW = 4
-DOC_ROWS = 16
+DOC_ROWS = 8
 PACK_ROWS = TOK + DOC_ROWS
 PACK_COLS = 1280
 HALF = D // 2

time: 203 us -> 202 us (level)
  blocking collectives: 63.2 us -> 60.9 us
    ppermute x2, waiting for transfers between devices: 14.2 us -> 17.5 us  [go_right(): return lax.ppermute(v, 'ctx', RIGHT)]
where the time goes in v3:
time: 202 us
  waiting for transfers between devices  62.3 us (31%)
  blocking collectives  60.9 us (30%)
  Pallas kernels  37.3 us (18%)
  starting transfers between devices  37.1 us (18%)
  local copies, waits for them, and re-layouts  3.37 us (2%)
    ppermute x16, waiting for transfers between devices, permute(): return lax.ppermute(v, ('ctx', 'exp'), pairs)  42.9 us
    ppermute x16, starting transfers between devices, permute(): return lax.ppermute(v, ('ctx', 'exp'), pairs)  29.1 us
    all_to_all x1, blocking collectives, on_device(): lax.all_to_all(summed, 'exp', split_axis=0, concat_axis=0, tiled=True)  22.1 us
    all_to_all x1, blocking collectives, on_device(): lax.all_to_all(packed, 'ctx', split_axis=0, concat_axis=0, tiled=True, ax...  19.5 us
    all_to_all x1, blocking collectives, on_device(): lax.all_to_all(send, 'exp', split_axis=0, concat_axis=0, tiled=True)  19.3 us
    ppermute x2, waiting for transfers between devices, go_right(): return lax.ppermute(v, 'ctx', RIGHT)  17.5 us
    pallas_call x4, Pallas kernels, experts(): pl.pallas_call(functools.partial(expert_kernel, sizes, near), out_shape=t...  16.4 us
    pallas_call x3, Pallas kernels, attend(): pl.pallas_call(functools.partial(attend_kernel, steps), out_shape=jax.Sha...  12.5 us
  transfers between devices with their start and end apart: 21, of which 13 were waited for; matrix products, arithmetic and copies ran while one was open for 0% of the time, Pallas kernels for 16%

profile of v3, /device:TPU:1, one launch (start us, length us, event | category | flops | bytes accessed | tf_op | source)
XLA Modules:
  0.0 202.0 jit_solution(14779963452389749885)
XLA Ops:
  0.0 1.6 dynamic-slice_bitcast_fusion
  1.7 0.4 copy-done.3
  2.0 0.8 collective-permute-start
  2.8 3.6 %collective-permute-start.2 = (bf16[1440,512]{1,0:T(8,128)(2,1)S(1)}, bf16[1440,512]{1,0:T(8,128)(2,1)S(1)}, u32[]{:S(2)}, u32[]{:S(2)}) collective-permute-start(bf16[1440,512]{1,0:T(8,128)(2,1)S(1)} %dynamic-slice_bitcast_fusion), channel_id=1, source_target_pairs={{0,66},{1,67},{2,64},{3,65},{4,70},{5,71},{6,68},{7,69},{8,74},{9,... | collective-permute-start | bytes 4423688 | tf_op jit(solution)/shard_map/ppermute | solution.py:484
  6.5 1.2 copy-done.4
  7.7 0.2 shard_map.127
  7.9 0.0 copy-start.1
  7.9 19.5 %all_to_all.28.pack_ref = bf16[4,136,1280]{2,1,0:T(8,128)(2,1)S(1)} all-to-all(bf16[4,136,1280]{2,1,0:T(8,128)(2,1)S(1)} %shard_map.127), channel_id=1, replica_groups={{0,16,32,48},{64,80,96,112},{1,17,33,49},{65,81,97,113},{2,18,34,50},{6..., dimensions={0} | all-to-all | bytes 2785280 | tf_op jit(solution)/shard_map/all_to_all | solution.py:548
  27.5 1.5 collective-permute-start.1
  29.0 2.3 %collective-permute-start.4 = (bf16[360,2880]{1,0:T(8,128)(2,1)S(1)}, bf16[360,2880]{1,0:T(8,128)(2,1)S(1)}, u32[]{:S(2)}, u32[]{:S(2)}) collective-permute-start(bf16[360,2880]{1,0:T(8,128)(2,1)S(1)} %bitcast.56), channel_id=1, source_target_pairs={{1,17},{3,19},{5,21},{7,23},{9,25},{11,27},{13,29},{15,31},{17,1},... | collective-permute-start | bytes 6220808 | tf_op jit(solution)/shard_map/ppermute | solution.py:484
  31.3 0.3 shard_map.128
  31.6 3.9 %collective-permute-done.2.w_first = bf16[1440,512]{1,0:T(8,128)(2,1)S(1)} collective-permute-done((bf16[1440,512]{1,0:T(8,128)(2,1)S(1)}, bf16[1440,512]{1,0:T(8,128)(2,1)S(1)}, u32[]{:S(2)}, u32[]{:S(2)}) %collective-permute-start.2) | collective-permute-done | bytes 1474592 | tf_op jit(solution)/shard_map/ppermute | solution.py:484
  35.5 4.6 %collective-permute-start.3 = (bf16[1440,512]{1,0:T(8,128)(2,1)S(1)}, bf16[1440,512]{1,0:T(8,128)(2,1)S(1)}, u32[]{:S(2)}, u32[]{:S(2)}) collective-permute-start(bf16[1440,512]{1,0:T(8,128)(2,1)S(1)} %collective-permute-done.2.w_first), channel_id=1, source_target_pairs={{0,1},{1,0},{2,3},{3,2},{4,5},{5,4},{6,7},{7,6},{8,9},{9,8},{10,11... | collective-permute-start | bytes 4423688 | tf_op jit(solution)/shard_map/ppermute | solution.py:484
  40.1 0.9 collective-permute-start.9
  41.0 3.5 %shard_map.129.attn = bf16[128,1024]{1,0:T(8,128)(2,1)S(1)} custom-call(f32[64]{0:T(128)S(1)} %copy-done.11, bf16[4,136,1280]{2,1,0:T(8,128)(2,1)S(1)} %all_to_all.28.pack_ref, bf16[4,136,256]{2,1,0:T(8,128)(2,1)S(1)} %collective-permute-done.1.low_ref), custom_call_target="tpu_custom_call" | custom-call | flops 2147483648 | bytes 4194304 | tf_op jit(solution)/shard_map/pallas_call | solution.py:209
  44.6 1.7 shard_map.130
  46.3 2.1 %collective-permute-start.5 = (bf16[1440,128]{1,0:T(8,128)(2,1)S(1)}, bf16[1440,128]{1,0:T(8,128)(2,1)S(1)}, u32[]{:S(2)}, u32[]{:S(2)}) collective-permute-start(bf16[1440,128]{1,0:T(8,128)(2,1)S(1)} %get-tuple-element.99), channel_id=1, source_target_pairs={{0,16},{16,32},{32,48},{48,0},{64,80},{80,96},{96,112},{112,64},{1... | collective-permute-start | bytes 1105928 | tf_op jit(solution)/shard_map/ppermute | solution.py:41
  48.4 1.6 collective-permute-start.6
  50.0 6.0 %shard_map.131.attn = bf16[256,1024]{1,0:T(8,128)(2,1)S(1)} custom-call(f32[64]{0:T(128)S(1)} %copy-done.11, bf16[4,136,1280]{2,1,0:T(8,128)(2,1)S(1)} %all_to_all.28.pack_ref, bf16[4,136,256]{2,1,0:T(8,128)(2,1)S(1)} %collective-permute-done.1.low_ref), custom_call_target="tpu_custom_call" | custom-call | flops 2147483648 | bytes 4194304 | tf_op jit(solution)/shard_map/pallas_call | solution.py:209
  56.0 1.0 collective-permute-done.4.refs_3_.refs_7_
  57.0 5.4 %collective-permute-done.5.refs_0_ = bf16[1440,128]{1,0:T(8,128)(2,1)S(1)} collective-permute-done((bf16[1440,128]{1,0:T(8,128)(2,1)S(1)}, bf16[1440,128]{1,0:T(8,128)(2,1)S(1)}, u32[]{:S(2)}, u32[]{:S(2)}) %collective-permute-start.5) | collective-permute-done | bytes 368672 | tf_op jit(solution)/shard_map/ppermute | solution.py:41
  62.4 1.8 collective-permute-done.6.refs_1_
  64.2 1.8 shard_map.132
  66.0 0.4 collective-permute-start.7
  66.5 2.3 %collective-permute-start.8 = (bf16[2880,128]{1,0:T(8,128)(2,1)S(1)}, bf16[2880,128]{1,0:T(8,128)(2,1)S(1)}, u32[]{:S(2)}, u32[]{:S(2)}) collective-permute-start(bf16[2880,128]{1,0:T(8,128)(2,1)S(1)} %get-tuple-element.104), channel_id=1, source_target_pairs={{0,48},{16,0},{32,16},{48,32},{64,112},{80,64},{96,80},{112,96},{1... | collective-permute-start | bytes 2211848 | tf_op jit(solution)/shard_map/ppermute | solution.py:45
  68.8 3.0 %shard_map.133.attn = bf16[128,1024]{1,0:T(8,128)(2,1)S(1)} custom-call(f32[64]{0:T(128)S(1)} %copy-done.11, bf16[4,136,1280]{2,1,0:T(8,128)(2,1)S(1)} %all_to_all.28.pack_ref, bf16[4,136,256]{2,1,0:T(8,128)(2,1)S(1)} %collective-permute-done.1.low_ref), custom_call_target="tpu_custom_call" | custom-call | flops 2147483648 | bytes 4194304 | tf_op jit(solution)/shard_map/pallas_call | solution.py:209
  71.8 0.0 copy-start.5
  71.9 0.0 copy-start.8
  71.9 1.7 shard_map.134
  73.5 12.1 %collective-permute-done.7.left = bf16[2880,128]{1,0:T(8,128)(2,1)S(1)} collective-permute-done((bf16[2880,128]{1,0:T(8,128)(2,1)S(1)}, bf16[2880,128]{1,0:T(8,128)(2,1)S(1)}, u32[]{:S(2)}, u32[]{:S(2)}) %collective-permute-start.7) | collective-permute-done | bytes 737312 | tf_op jit(solution)/shard_map/ppermute | solution.py:41
  85.6 1.9 collective-permute-start.16
  87.6 1.2 shard_map.135
  88.7 19.3 %all_to_all.29 = bf16[16,8,2880]{2,1,0:T(8,128)(2,1)S(1)} all-to-all(bf16[16,8,2880]{2,1,0:T(8,128)(2,1)S(1)} %bitcast.60), channel_id=1, replica_groups=mesh['ctx'=8,'exp'=16] {'exp'}, dimensions={0} | all-to-all | bytes 1474560 | tf_op jit(solution)/shard_map/all_to_all | solution.py:581
  108.0 0.1 fusion.4
  108.1 0.1 collective-permute-start.12
  108.2 2.7 %collective-permute-start.10 = (bf16[64,2880]{1,0:T(8,128)(2,1)S(1)}, bf16[64,2880]{1,0:T(8,128)(2,1)S(1)}, u32[]{:S(2)}, u32[]{:S(2)}) collective-permute-start(bf16[64,2880]{1,0:T(8,128)(2,1)S(1)} %get-tuple-element.147.refs_0_), channel_id=1, source_target_pairs={{0,16},{1,49},{2,18},{3,51},{4,20},{5,53},{6,22},{7,55},{8,24},{9,... | collective-permute-start | bytes 1105928 | tf_op jit(solution)/shard_map/ppermute | solution.py:484
  110.8 1.3 collective-permute-start.14
  112.1 0.2 collective-permute-start.15
  112.3 3.5 %collective-permute-done.12.refs_3_ = bf16[64,2880]{1,0:T(8,128)(2,1)S(1)} collective-permute-done((bf16[64,2880]{1,0:T(8,128)(2,1)S(1)}, bf16[64,2880]{1,0:T(8,128)(2,1)S(1)}, u32[]{:S(2)}, u32[]{:S(2)}) %collective-permute-start.12) | collective-permute-done | bytes 368672 | tf_op jit(solution)/shard_map/ppermute | solution.py:484
  115.8 2.0 %collective-permute-start.13 = (bf16[64,2880]{1,0:T(8,128)(2,1)S(1)}, bf16[64,2880]{1,0:T(8,128)(2,1)S(1)}, u32[]{:S(2)}, u32[]{:S(2)}) collective-permute-start(bf16[64,2880]{1,0:T(8,128)(2,1)S(1)} %collective-permute-done.12.refs_3_), channel_id=1, source_target_pairs={{16,0},{49,1},{18,2},{51,3},{20,4},{53,5},{22,6},{55,7},{24,8},{57... | collective-permute-start | bytes 1105928 | tf_op jit(solution)/shard_map/ppermute | solution.py:484
  117.8 0.5 collective-permute-done.10.refs_2_
  118.3 3.4 %collective-permute-start.11 = (bf16[64,2880]{1,0:T(8,128)(2,1)S(1)}, bf16[64,2880]{1,0:T(8,128)(2,1)S(1)}, u32[]{:S(2)}, u32[]{:S(2)}) collective-permute-start(bf16[64,2880]{1,0:T(8,128)(2,1)S(1)} %collective-permute-done.10.refs_2_), channel_id=1, source_target_pairs={{0,16},{1,49},{2,18},{3,51},{4,20},{5,53},{6,22},{7,55},{8,24},{9,... | collective-permute-start | bytes 1105928 | tf_op jit(solution)/shard_map/ppermute | solution.py:484
  121.7 3.4 %shard_map.136 = (bf16[64,2880]{1,0:T(8,128)(2,1)S(1)}, bf16[64,2880]{1,0:T(8,128)(2,1)S(1)}, bf16[64,2880]{1,0:T(8,128)(2,1)S(1)}, bf16[64,2880]{1,0:T(8,128)(2,1)S(1)}) custom-call(bf16[64,2880]{1,0:T(8,128)(2,1)S(1)} %get-tuple-element.147.refs_0_, bf16[64,2880]{1,0:T(8,128)(2,1)S(1)} %get-tuple-element.148.refs_1_, ...), custom_call_target="tpu_custom_call" | custom-call | flops 1592524800 | bytes 4194304 | tf_op jit(solution)/shard_map/pallas_call | solution.py:441
  125.1 1.3 collective-permute-done.14.refs_2_.refs_4_
  126.4 5.8 %collective-permute-done.13.refs_1_ = bf16[64,2880]{1,0:T(8,128)(2,1)S(1)} collective-permute-done((bf16[64,2880]{1,0:T(8,128)(2,1)S(1)}, bf16[64,2880]{1,0:T(8,128)(2,1)S(1)}, u32[]{:S(2)}, u32[]{:S(2)}) %collective-permute-start.13) | collective-permute-done | bytes 368672 | tf_op jit(solution)/shard_map/ppermute | solution.py:484
  132.2 2.3 %collective-permute-done.11.refs_0_ = bf16[64,2880]{1,0:T(8,128)(2,1)S(1)} collective-permute-done((bf16[64,2880]{1,0:T(8,128)(2,1)S(1)}, bf16[64,2880]{1,0:T(8,128)(2,1)S(1)}, u32[]{:S(2)}, u32[]{:S(2)}) %collective-permute-start.11) | collective-permute-done | bytes 368672 | tf_op jit(solution)/shard_map/ppermute | solution.py:484
  134.4 3.4 %shard_map.137 = (bf16[64,2880]{1,0:T(8,128)(2,1)S(1)}, bf16[64,2880]{1,0:T(8,128)(2,1)S(1)}, bf16[64,2880]{1,0:T(8,128)(2,1)S(1)}, bf16[64,2880]{1,0:T(8,128)(2,1)S(1)}) custom-call(bf16[64,2880]{1,0:T(8,128)(2,1)S(1)} %collective-permute-done.11.refs_0_, bf16[64,2880]{1,0:T(8,128)(2,1)S(1)} %collective-permute-done.13.refs_1_, ...), custom_call_target="tpu_custom_call" | custom-call | flops 1592524800 | bytes 4194304 | tf_op jit(solution)/shard_map/pallas_call | solution.py:441
  137.9 10.1 %collective-permute-done.16.refs_5_.refs_9_ = bf16[728,2880]{1,0:T(8,128)(2,1)S(1)} collective-permute-done((bf16[728,2880]{1,0:T(8,128)(2,1)S(1)}, bf16[728,2880]{1,0:T(8,128)(2,1)S(1)}, u32[]{:S(2)}, u32[]{:S(2)}) %collective-permute-start.16) | collective-permute-done | bytes 4193312 | tf_op jit(solution)/shard_map/ppermute | solution.py:484
  147.9 3.4 %shard_map.138 = (bf16[64,2880]{1,0:T(8,128)(2,1)S(1)}, bf16[64,2880]{1,0:T(8,128)(2,1)S(1)}) custom-call(bf16[64,2880]{1,0:T(8,128)(2,1)S(1)} %collective-permute-done.11.refs_0_, bf16[64,2880]{1,0:T(8,128)(2,1)S(1)} %collective-permute-done.13.refs_1_, bf16[360,2880]{1,0:T(8,128)(2,1)S(1)} %collective-permute-done.refs_2_.refs_6_, ...), custom_call_target="tpu_custom_call" | custom-call | flops 796262400 | bytes 4194304 | tf_op jit(solution)/shard_map/pallas_call | solution.py:441
  151.4 2.5 %collective-permute-start.17 = (bf16[64,2880]{1,0:T(8,128)(2,1)S(1)}, bf16[64,2880]{1,0:T(8,128)(2,1)S(1)}, u32[]{:S(2)}, u32[]{:S(2)}) collective-permute-start(bf16[64,2880]{1,0:T(8,128)(2,1)S(1)} %get-tuple-element.145), channel_id=1, source_target_pairs={{0,16},{1,49},{2,18},{3,51},{4,20},{5,53},{6,22},{7,55},{8,24},{9,... | collective-permute-start | bytes 1105928 | tf_op jit(solution)/shard_map/ppermute | solution.py:484
  153.9 6.1 %shard_map.139 = (bf16[64,2880]{1,0:T(8,128)(2,1)S(1)}, bf16[64,2880]{1,0:T(8,128)(2,1)S(1)}, bf16[64,2880]{1,0:T(8,128)(2,1)S(1)}, bf16[64,2880]{1,0:T(8,128)(2...) custom-call(bf16[64,2880]{1,0:T(8,128)(2,1)S(1)} %get-tuple-element.147.refs_0_, ...), custom_call_target="tpu_custom_call" | custom-call | flops 2388787200 | bytes 4194304 | tf_op jit(solution)/shard_map/pallas_call | solution.py:441
  160.1 1.5 collective-permute-done.18
  161.6 0.1 fusion.3
  161.7 0.1 pad_maximum_fusion.1
  161.8 0.1 collective-permute-start.20
  161.9 0.1 fusion.2
  162.0 0.1 pad_maximum_fusion
  162.1 2.7 %collective-permute-start.19 = (bf16[2,64,2880]{2,1,0:T(8,128)(2,1)S(1)}, bf16[2,64,2880]{2,1,0:T(8,128)(2,1)S(1)}, u32[]{:S(2)}, u32[]{:S(2)}) collective-permute-start(bf16[2,64,2880]{2,1,0:T(8,128)(2,1)S(1)} %pad_maximum_fusion), channel_id=1, source_target_pairs={{0,16},{1,49},{2,18},{3,51},{4,20},{5,53},{6,22},{7,55},{8,24},{9,... | collective-permute-start | bytes 2211848 | tf_op jit(solution)/shard_map/ppermute | solution.py:484
  164.8 13.2 %collective-permute-done.20 = bf16[2,64,2880]{2,1,0:T(8,128)(2,1)S(1)} collective-permute-done((bf16[2,64,2880]{2,1,0:T(8,128)(2,1)S(1)}, bf16[2,64,2880]{2,1,0:T(8,128)(2,1)S(1)}, u32[]{:S(2)}, u32[]{:S(2)}) %collective-permute-start.20) | collective-permute-done | bytes 737312 | tf_op jit(solution)/shard_map/ppermute | solution.py:484
  178.0 0.3 fusion.1
  178.2 0.0 copy-start.9
  178.3 0.1 maximum_bitcast_fusion
  178.3 22.1 %all_to_all.30 = bf16[16,8,2880]{2,1,0:T(8,128)(2,1)S(1)} all-to-all(bf16[16,8,2880]{2,1,0:T(8,128)(2,1)S(1)} %maximum_bitcast_fusion), channel_id=1, replica_groups=mesh['ctx'=8,'exp'=16] {'exp'}, dimensions={0} | all-to-all | bytes 1474560 | tf_op jit(solution)/shard_map/all_to_all | solution.py:584
  200.4 1.6 shard_map.140
  (31 shorter events, 0.1 us)
Async XLA Ops:
  0.0 2.0 %copy-start.3 = (bf16[1,2880,360]{1,2,0:T(8,128)(2,1)S(1)}, bf16[1,2880,360]{1,2,0:T(8,128)(2,1)}, u32[]{:S(2)}) copy-start(bf16[1,2880,360]{1,2,0:T(8,128)(2,1)} %param.21) | copy-start | bytes 6220804
  0.0 6.5 %copy-start.10 = (s32[128]{0:T(128)S(1)}, s32[128]{0:T(128)}, u32[]{:S(2)}) copy-start(s32[128]{0:T(128)} %param.18) | copy-start | bytes 1540
  0.0 6.5 %copy-start.7 = (bf16[128,512]{1,0:T(8,128)(2,1)S(1)}, bf16[128,512]{1,0:T(8,128)(2,1)}, u32[]{:S(2)}) copy-start(bf16[128,512]{1,0:T(8,128)(2,1)} %v_ref.1) | copy-start | bytes 393220
  0.0 6.5 %copy-start.6 = (bf16[128,512]{1,0:T(8,128)(2,1)S(1)}, bf16[128,512]{1,0:T(8,128)(2,1)}, u32[]{:S(2)}) copy-start(bf16[128,512]{1,0:T(8,128)(2,1)} %k_ref.1) | copy-start | bytes 393220
  2.0 25.4 %collective-permute-start = (bf16[360,2880]{1,0:T(8,128)(2,1)S(1)}, bf16[360,2880]{1,0:T(8,128)(2,1)S(1)}, u32[]{:S(2)}, u32[]{:S(2)}) collective-permute-start(bf16[360,2880]{1,0:T(8,128)(2,1)S(1)} %bitcast.55), channel_id=1, source_target_pairs={{0,64},{2,66},{4,68},{6,70},{8,72},{10,74},{12,76},{14,78},{16,80}... | collective-permute-start | bytes 6220808 | tf_op jit(solution)/shard_map/ppermute | solution.py:484
  2.8 32.7 %collective-permute-start.2 = (bf16[1440,512]{1,0:T(8,128)(2,1)S(1)}, bf16[1440,512]{1,0:T(8,128)(2,1)S(1)}, u32[]{:S(2)}, u32[]{:S(2)}) collective-permute-start(bf16[1440,512]{1,0:T(8,128)(2,1)S(1)} %dynamic-slice_bitcast_fusion), channel_id=1, source_target_pairs={{0,66},{1,67},{2,64},{3,65},{4,70},{5,71},{6,68},{7,69},{8,74},{9,... | collective-permute-start | bytes 4423688 | tf_op jit(solution)/shard_map/ppermute | solution.py:484
  6.5 1.2 copy-start.4
  7.7 23.6 %copy-start.2 = (bf16[1,360,2880]{2,1,0:T(8,128)(2,1)S(1)}, bf16[1,360,2880]{2,1,0:T(8,128)(2,1)}, u32[]{:S(2)}) copy-start(bf16[1,360,2880]{2,1,0:T(8,128)(2,1)} %param.23) | copy-start | bytes 6220804
  7.9 23.4 %copy-start.1 = (bf16[1,2880,360]{1,2,0:T(8,128)(2,1)S(1)}, bf16[1,2880,360]{1,2,0:T(8,128)(2,1)}, u32[]{:S(2)}) copy-start(bf16[1,2880,360]{1,2,0:T(8,128)(2,1)} %param.22) | copy-start | bytes 6220804
  27.5 8.0 %collective-permute-start.1 = (bf16[4,136,256]{2,1,0:T(8,128)(2,1)S(1)}, bf16[4,136,256]{2,1,0:T(8,128)(2,1)S(1)}, u32[]{:S(2)}, u32[]{:S(2)}) collective-permute-start(bf16[4,136,256]{2,1,0:T(8,128)(2,1)S(1)} %slice.21), channel_id=1, source_target_pairs={{0,64},{16,80},{32,96},{48,112},{1,65},{17,81},{33,97},{49,113},{2... | collective-permute-start | bytes 835592 | tf_op jit(solution)/shard_map/ppermute | solution.py:557
  29.0 28.0 %collective-permute-start.4 = (bf16[360,2880]{1,0:T(8,128)(2,1)S(1)}, bf16[360,2880]{1,0:T(8,128)(2,1)S(1)}, u32[]{:S(2)}, u32[]{:S(2)}) collective-permute-start(bf16[360,2880]{1,0:T(8,128)(2,1)S(1)} %bitcast.56), channel_id=1, source_target_pairs={{1,17},{3,19},{5,21},{7,23},{9,25},{11,27},{13,29},{15,31},{17,1},... | collective-permute-start | bytes 6220808 | tf_op jit(solution)/shard_map/ppermute | solution.py:484
  31.3 9.7 %copy-start.11 = (f32[64]{0:T(128)S(1)}, f32[64]{0:T(128)}, u32[]{:S(2)}) copy-start(f32[64]{0:T(128)} %sinks.5) | copy-start | bytes 772
  31.6 12.9 %copy-start = (bf16[512,2880]{0,1:T(8,128)(2,1)S(1)}, bf16[512,2880]{0,1:T(8,128)(2,1)}, u32[]{:S(2)}) copy-start(bf16[512,2880]{0,1:T(8,128)(2,1)} %param.20) | copy-start | bytes 8847364
  35.5 9.0 %collective-permute-start.3 = (bf16[1440,512]{1,0:T(8,128)(2,1)S(1)}, bf16[1440,512]{1,0:T(8,128)(2,1)S(1)}, u32[]{:S(2)}, u32[]{:S(2)}) collective-permute-start(bf16[1440,512]{1,0:T(8,128)(2,1)S(1)} %collective-permute-done.2.w_first), channel_id=1, source_target_pairs={{0,1},{1,0},{2,3},{3,2},{4,5},{5,4},{6,7},{7,6},{8,9},{9,8},{10,11... | collective-permute-start | bytes 4423688 | tf_op jit(solution)/shard_map/ppermute | solution.py:484
  40.1 67.9 %collective-permute-start.9 = (bf16[728,2880]{1,0:T(8,128)(2,1)S(1)}, bf16[728,2880]{1,0:T(8,128)(2,1)S(1)}, u32[]{:S(2)}, u32[]{:S(2)}) collective-permute-start(bf16[728,2880]{1,0:T(8,128)(2,1)S(1)} %shard_map.128), channel_id=1, source_target_pairs={{0,64},{2,66},{4,68},{6,70},{8,72},{10,74},{12,76},{14,78},{16,80}... | collective-permute-start | bytes 12579848 | tf_op jit(solution)/shard_map/ppermute | solution.py:484
  46.3 16.1 %collective-permute-start.5 = (bf16[1440,128]{1,0:T(8,128)(2,1)S(1)}, bf16[1440,128]{1,0:T(8,128)(2,1)S(1)}, u32[]{:S(2)}, u32[]{:S(2)}) collective-permute-start(bf16[1440,128]{1,0:T(8,128)(2,1)S(1)} %get-tuple-element.99), channel_id=1, source_target_pairs={{0,16},{16,32},{32,48},{48,0},{64,80},{80,96},{96,112},{112,64},{1... | collective-permute-start | bytes 1105928 | tf_op jit(solution)/shard_map/ppermute | solution.py:41
  48.4 15.8 %collective-permute-start.6 = (bf16[1440,128]{1,0:T(8,128)(2,1)S(1)}, bf16[1440,128]{1,0:T(8,128)(2,1)S(1)}, u32[]{:S(2)}, u32[]{:S(2)}) collective-permute-start(bf16[1440,128]{1,0:T(8,128)(2,1)S(1)} %get-tuple-element.100), channel_id=1, source_target_pairs={{0,48},{16,0},{32,16},{48,32},{64,112},{80,64},{96,80},{112,96},{1... | collective-permute-start | bytes 1105928 | tf_op jit(solution)/shard_map/ppermute | solution.py:45
  66.0 19.6 %collective-permute-start.7 = (bf16[2880,128]{1,0:T(8,128)(2,1)S(1)}, bf16[2880,128]{1,0:T(8,128)(2,1)S(1)}, u32[]{:S(2)}, u32[]{:S(2)}) collective-permute-start(bf16[2880,128]{1,0:T(8,128)(2,1)S(1)} %get-tuple-element.103), channel_id=1, source_target_pairs={{0,16},{16,32},{32,48},{48,0},{64,80},{80,96},{96,112},{112,64},{1... | collective-permute-start | bytes 2211848 | tf_op jit(solution)/shard_map/ppermute | solution.py:41
  66.5 19.1 %collective-permute-start.8 = (bf16[2880,128]{1,0:T(8,128)(2,1)S(1)}, bf16[2880,128]{1,0:T(8,128)(2,1)S(1)}, u32[]{:S(2)}, u32[]{:S(2)}) collective-permute-start(bf16[2880,128]{1,0:T(8,128)(2,1)S(1)} %get-tuple-element.104), channel_id=1, source_target_pairs={{0,48},{16,0},{32,16},{48,32},{64,112},{80,64},{96,80},{112,96},{1... | collective-permute-start | bytes 2211848 | tf_op jit(solution)/shard_map/ppermute | solution.py:45
  71.8 15.7 %copy-start.12 = (f32[2880]{0:T(1024)S(1)}, f32[2880]{0:T(1024)}, u32[]{:S(2)}) copy-start(f32[2880]{0:T(1024)} %param.19) | copy-start | bytes 34564
  71.8 15.7 %copy-start.5 = (bf16[128,2880]{0,1:T(8,128)(2,1)S(1)}, bf16[128,2880]{0,1:T(8,128)(2,1)}, u32[]{:S(2)}) copy-start(bf16[128,2880]{0,1:T(8,128)(2,1)} %param.13) | copy-start | bytes 2211844
  71.9 15.7 %copy-start.8 = (s32[128,4]{0,1:T(4,128)S(1)}, s32[128,4]{0,1:T(4,128)}, u32[]{:S(2)}) copy-start(s32[128,4]{0,1:T(4,128)} %param.24) | copy-start | bytes 6148
  85.6 62.3 %collective-permute-start.16 = (bf16[728,2880]{1,0:T(8,128)(2,1)S(1)}, bf16[728,2880]{1,0:T(8,128)(2,1)S(1)}, u32[]{:S(2)}, u32[]{:S(2)}) collective-permute-start(bf16[728,2880]{1,0:T(8,128)(2,1)S(1)} %shard_map.128), channel_id=1, source_target_pairs={{1,17},{3,19},{5,21},{7,23},{9,25},{11,27},{13,29},{15,31},{17,1},... | collective-permute-start | bytes 12579848 | tf_op jit(solution)/shard_map/ppermute | solution.py:484
  108.1 7.7 %collective-permute-start.12 = (bf16[64,2880]{1,0:T(8,128)(2,1)S(1)}, bf16[64,2880]{1,0:T(8,128)(2,1)S(1)}, u32[]{:S(2)}, u32[]{:S(2)}) collective-permute-start(bf16[64,2880]{1,0:T(8,128)(2,1)S(1)} %get-tuple-element.148.refs_1_), channel_id=1, source_target_pairs={{16,0},{49,1},{18,2},{51,3},{20,4},{53,5},{22,6},{55,7},{24,8},{57... | collective-permute-start | bytes 1105928 | tf_op jit(solution)/shard_map/ppermute | solution.py:484
  108.2 10.1 %collective-permute-start.10 = (bf16[64,2880]{1,0:T(8,128)(2,1)S(1)}, bf16[64,2880]{1,0:T(8,128)(2,1)S(1)}, u32[]{:S(2)}, u32[]{:S(2)}) collective-permute-start(bf16[64,2880]{1,0:T(8,128)(2,1)S(1)} %get-tuple-element.147.refs_0_), channel_id=1, source_target_pairs={{0,16},{1,49},{2,18},{3,51},{4,20},{5,53},{6,22},{7,55},{8,24},{9,... | collective-permute-start | bytes 1105928 | tf_op jit(solution)/shard_map/ppermute | solution.py:484
  110.8 15.5 %collective-permute-start.14 = (bf16[64,2880]{1,0:T(8,128)(2,1)S(1)}, bf16[64,2880]{1,0:T(8,128)(2,1)S(1)}, u32[]{:S(2)}, u32[]{:S(2)}) collective-permute-start(bf16[64,2880]{1,0:T(8,128)(2,1)S(1)} %get-tuple-element.148.refs_1_), channel_id=1, source_target_pairs={{0,16},{1,49},{2,18},{3,51},{4,20},{5,53},{6,22},{7,55},{8,24},{9,... | collective-permute-start | bytes 1105928 | tf_op jit(solution)/shard_map/ppermute | solution.py:484
  112.1 14.3 %collective-permute-start.15 = (bf16[64,2880]{1,0:T(8,128)(2,1)S(1)}, bf16[64,2880]{1,0:T(8,128)(2,1)S(1)}, u32[]{:S(2)}, u32[]{:S(2)}) collective-permute-start(bf16[64,2880]{1,0:T(8,128)(2,1)S(1)} %get-tuple-element.147.refs_0_), channel_id=1, source_target_pairs={{16,0},{49,1},{18,2},{51,3},{20,4},{53,5},{22,6},{55,7},{24,8},{57... | collective-permute-start | bytes 1105928 | tf_op jit(solution)/shard_map/ppermute | solution.py:484
  115.8 16.4 %collective-permute-start.13 = (bf16[64,2880]{1,0:T(8,128)(2,1)S(1)}, bf16[64,2880]{1,0:T(8,128)(2,1)S(1)}, u32[]{:S(2)}, u32[]{:S(2)}) collective-permute-start(bf16[64,2880]{1,0:T(8,128)(2,1)S(1)} %collective-permute-done.12.refs_3_), channel_id=1, source_target_pairs={{16,0},{49,1},{18,2},{51,3},{20,4},{53,5},{22,6},{55,7},{24,8},{57... | collective-permute-start | bytes 1105928 | tf_op jit(solution)/shard_map/ppermute | solution.py:484
  118.3 16.2 %collective-permute-start.11 = (bf16[64,2880]{1,0:T(8,128)(2,1)S(1)}, bf16[64,2880]{1,0:T(8,128)(2,1)S(1)}, u32[]{:S(2)}, u32[]{:S(2)}) collective-permute-start(bf16[64,2880]{1,0:T(8,128)(2,1)S(1)} %collective-permute-done.10.refs_2_), channel_id=1, source_target_pairs={{0,16},{1,49},{2,18},{3,51},{4,20},{5,53},{6,22},{7,55},{8,24},{9,... | collective-permute-start | bytes 1105928 | tf_op jit(solution)/shard_map/ppermute | solution.py:484
  151.4 8.7 %collective-permute-start.17 = (bf16[64,2880]{1,0:T(8,128)(2,1)S(1)}, bf16[64,2880]{1,0:T(8,128)(2,1)S(1)}, u32[]{:S(2)}, u32[]{:S(2)}) collective-permute-start(bf16[64,2880]{1,0:T(8,128)(2,1)S(1)} %get-tuple-element.145), channel_id=1, source_target_pairs={{0,16},{1,49},{2,18},{3,51},{4,20},{5,53},{6,22},{7,55},{8,24},{9,... | collective-permute-start | bytes 1105928 | tf_op jit(solution)/shard_map/ppermute | solution.py:484
  153.9 7.7 %collective-permute-start.18 = (bf16[64,2880]{1,0:T(8,128)(2,1)S(1)}, bf16[64,2880]{1,0:T(8,128)(2,1)S(1)}, u32[]{:S(2)}, u32[]{:S(2)}) collective-permute-start(bf16[64,2880]{1,0:T(8,128)(2,1)S(1)} %get-tuple-element.146), channel_id=1, source_target_pairs={{16,0},{49,1},{18,2},{51,3},{20,4},{53,5},{22,6},{55,7},{24,8},{57... | collective-permute-start | bytes 1105928 | tf_op jit(solution)/shard_map/ppermute | solution.py:484
  161.8 16.2 %collective-permute-start.20 = (bf16[2,64,2880]{2,1,0:T(8,128)(2,1)S(1)}, bf16[2,64,2880]{2,1,0:T(8,128)(2,1)S(1)}, u32[]{:S(2)}, u32[]{:S(2)}) collective-permute-start(bf16[2,64,2880]{2,1,0:T(8,128)(2,1)S(1)} %pad_maximum_fusion.1), channel_id=1, source_target_pairs={{16,0},{49,1},{18,2},{51,3},{20,4},{53,5},{22,6},{55,7},{24,8},{57... | collective-permute-start | bytes 2211848 | tf_op jit(solution)/shard_map/ppermute | solution.py:484
  162.1 15.9 %collective-permute-start.19 = (bf16[2,64,2880]{2,1,0:T(8,128)(2,1)S(1)}, bf16[2,64,2880]{2,1,0:T(8,128)(2,1)S(1)}, u32[]{:S(2)}, u32[]{:S(2)}) collective-permute-start(bf16[2,64,2880]{2,1,0:T(8,128)(2,1)S(1)} %pad_maximum_fusion), channel_id=1, source_target_pairs={{0,16},{1,49},{2,18},{3,51},{4,20},{5,53},{6,22},{7,55},{8,24},{9,... | collective-permute-start | bytes 2211848 | tf_op jit(solution)/shard_map/ppermute | solution.py:484
  178.2 22.1 %copy-start.9 = (f32[128,4]{0,1:T(4,128)S(1)}, f32[128,4]{0,1:T(4,128)}, u32[]{:S(2)}) copy-start(f32[128,4]{0,1:T(4,128)} %param.25) | copy-start | bytes 6148
